TPU v7x, 128 devices: a whole 4x4x4 slice. The times are simulated.
128 devices in a mesh: wn: 8 (over x, core), xz: 16 (over y, z).
Axes of the slice: x: 4, y: 4, z: 4, core: 2. Of those that a mesh axis runs over, the one named last changes fastest.
Arguments:
- velocity: float32 [3, 1024, 32, 2048], P(None, 'wn', None, 'xz'), may hold values from -3.5 to 3.5
- viscosity: float32 [1024, 32, 2048], P('wn', None, 'xz'), may hold values from 2 to 10
Outputs:
- new_velocity: float32 [3, 1024, 32, 2048], P(None, 'wn', None, 'xz')
All inputs are finite; a program needn't handle non-finite values.
Results may differ from a plain program's by a relative error of at most 0.0003.
Values sent between devices are 32-bit elements; how exact they have to be, the bound alone decides.
No kernel may reach another device: no remote copies, remote signals or barrier semaphores. Data moves between devices by JAX's collectives and lax.ppermute only.
A program may use at most 192 MiB of HBM per device.

v0:
```python
import jax
import jax.numpy as jnp
from jax import lax
from jax.sharding import PartitionSpec as P

x_courant = 0.25
y_courant = 0.5
z_courant = 0.25
diffusion_rate = 2000.0


def extended(cells, sides, width, closed):
    for axis, dim in sides:
        count = lax.axis_size(axis)
        ends = count if closed else count - 1
        head = lax.slice_in_dim(cells, 0, width, axis=dim)
        tail = lax.slice_in_dim(cells, cells.shape[dim] - width, cells.shape[dim], axis=dim)
        cells = jnp.concatenate(
            [
                lax.ppermute(tail, axis, [(i, (i + 1) % count) for i in range(ends)]),
                cells,
                lax.ppermute(head, axis, [((i + 1) % count, i) for i in range(ends)]),
            ],
            axis=dim,
        )
    return cells


def entering(x, axis, combine, identity, reverse):
    length, position = (lax.axis_size(axis), lax.axis_index(axis))
    everything = jax.tree.map(lambda part: lax.all_gather(part, axis), x)
    start = jax.tree.map(
        lambda part, zero: jnp.broadcast_to(jnp.asarray(zero, part.dtype), part.shape), x, identity
    )

    def turn(k, before):
        at = length - 1 - k if reverse else k
        reached = at > position if reverse else at < position
        new = combine(before, jax.tree.map(lambda part: part[at], everything))
        return jax.tree.map(lambda a, b: jnp.where(reached, a, b), new, before)

    return lax.fori_loop(0, length, turn, start)


def advect(velocity, diff_x, diff_y, diff_z):
    return velocity - (
        x_courant * velocity[0] * diff_x
        + y_courant * velocity[1] * diff_y
        + z_courant * velocity[2] * diff_z
    )


def thomas_rows(rhs, lower_rate, upper_rate):
    count_rows = rhs.shape[1]
    ratios = jnp.zeros(lower_rate.shape[1:], jnp.float32)
    values = jnp.zeros(rhs.shape[:1] + rhs.shape[2:], jnp.float32)
    saved = []
    for position in range(count_rows):
        lower_face = lower_rate[position]
        upper_face = upper_rate[position]
        pivots = 1.0 + lower_face + upper_face + lower_face * ratios
        ratios = -upper_face / pivots
        values = (rhs[:, position] + lower_face * values) / pivots
        saved.append((ratios, values))
    following = jnp.zeros_like(values)
    rows_out = []
    for position in reversed(range(count_rows)):
        following = saved[position][1] - saved[position][0] * following
        rows_out.append(following)
    return jnp.stack(rows_out[::-1], 1)


def join_blocks(left, right):
    denominator = 1.0 - left[4] * right[0]
    knot_value = (left[5] + left[4] * right[2]) / denominator
    knot_left = left[3] / denominator
    knot_right = left[4] * right[1] / denominator
    cross_value = right[2] + right[0] * knot_value
    cross_left = right[0] * knot_left
    cross_right = right[1] + right[0] * knot_right
    return (
        left[0] + left[1] * cross_left,
        left[1] * cross_right,
        left[2] + left[1] * cross_value,
        right[3] * knot_left,
        right[4] + right[3] * knot_right,
        right[5] + right[3] * knot_value,
    )


def flipped_join(earlier, later):
    return join_blocks(later, earlier)


def finish_block(values, left_reach, right_reach, summary, prefix, suffix):
    prefix_right = prefix[4]
    prefix_value = prefix[5]
    suffix_left = suffix[0]
    suffix_value = suffix[2]
    top_left = 1.0 - summary[0] * prefix_right
    top_right = -summary[1] * suffix_left
    bottom_left = -summary[3] * prefix_right
    bottom_right = 1.0 - summary[4] * suffix_left
    upper_source = summary[2] + summary[0] * prefix_value + summary[1] * suffix_value
    lower_source = summary[5] + summary[3] * prefix_value + summary[4] * suffix_value
    determinant = top_left * bottom_right - top_right * bottom_left
    first_cell = (upper_source * bottom_right - top_right * lower_source) / determinant
    last_cell = (top_left * lower_source - bottom_left * upper_source) / determinant
    left_neighbour = prefix_value + prefix_right * first_cell
    right_neighbour = suffix_value + suffix_left * last_cell
    return values + left_reach * left_neighbour[:, None] + right_reach * right_neighbour[:, None]


def local(velocity, viscosity):
    wide = extended(velocity, (("xz", 3),), 1, True)
    stacked = jnp.concatenate([velocity, viscosity[None]], 0)
    tall = extended(stacked, (("wn", 1),), 1, False)
    diff_x = jnp.roll(velocity, -1, 2) - jnp.roll(velocity, 1, 2)
    diff_y = tall[:3, 2:] - tall[:3, :-2]
    diff_z = wide[:, :, :, 2:] - wide[:, :, :, :-2]
    rhs = advect(velocity, diff_x, diff_y, diff_z)
    level = lax.axis_index("wn")
    devices_line = lax.axis_size("wn")
    rim_column = tall[3]
    below = jnp.concatenate(
        [jnp.where(level == 0, viscosity[:1], rim_column[:1]), rim_column[1:-2]], 0
    )
    above = jnp.concatenate(
        [rim_column[2:-1], jnp.where(level == devices_line - 1, viscosity[-1:], rim_column[-1:])], 0
    )
    lower_rate = diffusion_rate * 0.5 * (viscosity + below)
    upper_rate = diffusion_rate * 0.5 * (viscosity + above)
    unit_lower = jnp.concatenate([lower_rate[:1], jnp.zeros_like(lower_rate[1:])], 0)
    unit_upper = jnp.concatenate([jnp.zeros_like(upper_rate[:-1]), upper_rate[-1:]], 0)
    solved = thomas_rows(
        jnp.concatenate([rhs, unit_lower[None], unit_upper[None]], 0), lower_rate, upper_rate
    )
    values = solved[:3]
    left_reach = solved[3]
    right_reach = solved[4]
    summary = (
        left_reach[0],
        right_reach[0],
        values[:, 0],
        left_reach[-1],
        right_reach[-1],
        values[:, -1],
    )
    zeros_line = jnp.zeros_like(left_reach[0])
    ones_line = jnp.ones_like(left_reach[0])
    zeros_field = jnp.zeros_like(values[:, 0])
    identity = (zeros_line, ones_line, zeros_field, ones_line, zeros_line, zeros_field)
    prefix = entering(summary, "wn", join_blocks, identity, False)
    suffix = entering(summary, "wn", flipped_join, identity, True)
    return finish_block(values, left_reach, right_reach, summary, prefix, suffix)


def solution(mesh):
    placed = (P(None, "wn", None, "xz"), P("wn", None, "xz"))
    return jax.shard_map(
        local, mesh=mesh, in_specs=placed, out_specs=P(None, "wn", None, "xz"), check_vma=False
    )
```

profile of v0, /device:TPU:1, one launch (start us, length us, event | category | flops | bytes accessed | tf_op | source)
XLA Modules:
  0.0 280.2 jit_solution(949067484857253773)
XLA Ops:
  0.0 1.7 pad_maximum_fusion.8
  1.7 3.5 %collective-permute-start = (f32[4,1,32,128]{3,2,1,0:T(8,128)}, f32[4,1,32,128]{3,2,1,0:T(8,128)}, u32[]{:S(2)}, u32[]{:S(2)}) collective-permute-start(f32[4,1,32,128]{3,2,1,0:T(8,128)} %get-tuple-element.904), channel_id=1, source_target_pairs={{16,0},{32,16},{48,32},{64,48},{80,64},{96,80},{112,96},{17,1},{33... | collective-permute-start | bytes 196616 | tf_op jit(solution)/shard_map/ppermute | solution.py:22
  5.1 3.1 %collective-permute-start.1 = (f32[4,1,32,128]{3,2,1,0:T(8,128)}, f32[4,1,32,128]{3,2,1,0:T(8,128)}, u32[]{:S(2)}, u32[]{:S(2)}) collective-permute-start(f32[4,1,32,128]{3,2,1,0:T(8,128)} %get-tuple-element.905), channel_id=1, source_target_pairs={{0,16},{16,32},{32,48},{48,64},{64,80},{80,96},{96,112},{1,17},{17... | collective-permute-start | bytes 196616 | tf_op jit(solution)/shard_map/ppermute | solution.py:20
  8.2 7.0 %fusion.520 = (f32[3,128,32,1]{3,2,1,0:T(8,128)}, f32[3,128,32,1]{3,2,1,0:T(8,128)}) fusion(f32[3,128,32,128]{3,2,1,0:T(8,128)S(1)} %copy-done), kind=kLoop, calls=%fused_computation.1437 | loop fusion | bytes 196608 | tf_op jit(solution)/shard_map/slice | solution.py:16
  15.3 5.9 %copy.389 = f32[3,128,32,1]{1,2,3,0:T(8,128)} copy(f32[3,128,32,1]{3,2,1,0:T(8,128)} %get-tuple-element.913) | data formatting | bytes 98304
  21.2 6.2 %collective-permute-start.2 = (f32[3,128,32,1]{1,2,3,0:T(8,128)}, f32[3,128,32,1]{1,2,3,0:T(8,128)}, u32[]{:S(2)}, u32[]{:S(2)}) collective-permute-start(f32[3,128,32,1]{1,2,3,0:T(8,128)} %copy.389), channel_id=1, source_target_pairs={{1,0},{2,1},{3,2},{4,3},{5,4},{6,5},{7,6},{8,7},{9,8},{10,9},{11,1... | collective-permute-start | bytes 147464 | tf_op jit(solution)/shard_map/ppermute | solution.py:22
  27.4 5.9 %copy.390 = f32[3,128,32,1]{1,2,3,0:T(8,128)} copy(f32[3,128,32,1]{3,2,1,0:T(8,128)} %get-tuple-element.914) | data formatting | bytes 98304
  33.3 4.8 %slice_bitcast_fusion.2 = (f32[127,32,128]{2,1,0:T(8,128)}, f32[127,32,128]{2,1,0:T(8,128)}) fusion(f32[1,128,32,128]{3,2,1,0:T(8,128)} %bitcast.3952), kind=kLoop, calls=%fused_computation.60 | loop fusion | bytes 8323072 | tf_op jit(solution)/shard_map/slice | solution.py:129
  38.1 2.9 %multiply_bitcast_fusion.2 = (f32[128,32,128]{2,1,0:T(8,128)}, f32[128,32,128]{2,1,0:T(8,128)}, f32[128,32,128]{2,1,0:T(8,128)}) fusion(f32[3,128,32,128]{3,2,1,0:T(8,128)S(1)} %bitcast.3950), kind=kLoop, calls=%fused_computation.59 | loop fusion | flops 1572864 | bytes 12582912 | tf_op jit(solution)/shard_map/mul | solution.py:47
  41.0 6.3 %fusion.519 = (f32[3,128,31,128]{3,2,1,0:T(8,128)}, f32[3,128,31,128]{3,2,1,0:T(8,128)}) fusion(f32[3,128,32,128]{3,2,1,0:T(8,128)S(1)} %bitcast.3950), kind=kLoop, calls=%fused_computation.1436 | loop fusion | bytes 24379392 | tf_op jit(solution)/shard_map/jit(_roll_static)/slice | solution.py:118
  47.6 7.0 %copy.258 = f32[3,128,32,1]{3,2,1,0:T(8,128)} copy(f32[3,128,32,1]{1,2,3,0:T(8,128)} %collective-permute-done.2) | data formatting | bytes 98304 | tf_op jit(solution)/shard_map/ppermute | solution.py:22
  54.6 6.6 %copy.260 = f32[3,128,32,1]{3,2,1,0:T(8,128)} copy(f32[3,128,32,1]{1,2,3,0:T(8,128)} %collective-permute-done.3) | data formatting | bytes 98304 | tf_op jit(solution)/shard_map/ppermute | solution.py:20
  61.3 0.7 fusion.288
  62.0 3.6 %select_bitcast_fusion = (f32[1,128,32,128]{3,2,1,0:T(8,128)}, f32[128,32,128]{2,1,0:T(8,128)S(1)}, f32[128,32,128]{2,1,0:T(8,128)S(1)}) fusion(pred[128]{0:T(512)(128)(4,1)S(1)} %copy-done.125, f32[128,32,128]{2,1,0:T(8,128)S(1)} %copy-done.1, f32[127,32,128]{2,1,0:T(8,128)} %get-tuple-element.1069, f32[1,32,128]{2,1,0:T(8,128)S(1)} %get-tuple-element.1071, ...), kind=kLoop, calls=%fused_computation.56 | loop fusion | flops 3670016 | bytes 12583040 | tf_op jit(solution)/shard_map/broadcast_in_dim | solution.py:136
  65.7 0.7 slice_bitcast_fusion.324
  67.1 1.5 multiply_add_fusion.51
  68.6 0.8 slice_bitcast_fusion.326
  69.3 0.7 slice_bitcast_fusion.323
  70.8 0.7 slice_bitcast_fusion.325
  71.6 0.8 slice_bitcast_fusion.327
  85.9 1.6 pad_bitcast_fusion
  87.5 1.4 fusion.292
  88.9 27.0 %fusion.24 = f32[3,128,32,128]{3,2,1,0:T(8,128)} fusion(f32[3,128,32,128]{3,2,1,0:T(8,128)} %param.6, f32[3,128,32,1]{3,2,1,0:T(8,128)} %copy.260, f32[3,128,32,1]{3,2,1,0:T(8,128)} %copy.258, f32[4,1,32,128]{3,2,1,0:T(8,128)} %collective-permute-done.1, f32[1,128,32,128]{3,2,1,0:T(8,128)S(1)} %bitcast.3953, f32[4,1,32,128]{3,2,1,0:T(8,128)} %collective-permute-done, ...), kind=kLoop, calls=%fused_computation.38 | loop fusion | flops 26738688 | bytes 33783808 | tf_op jit(solution)/shard_map/sub | solution.py:46
  116.3 5.4 %pad_maximum_fusion = f32[5,128,32,128]{3,2,1,0:T(8,128)S(1)} fusion(f32[1,128,32,128]{3,2,1,0:T(8,128)} %pad_bitcast_fusion, f32[1,128,32,128]{3,2,1,0:T(8,128)} %get-tuple-element.900, f32[3,128,32,128]{3,2,1,0:T(8,128)} %fusion.24), kind=kLoop, calls=%fused_computation.31 | loop fusion | flops 5242880 | bytes 20971520 | tf_op jit(solution)/shard_map/concatenate | solution.py:136
  122.5 26.1 %multiply_subtract_fusion.100 = (f32[5,32,128]{2,1,0:T(8,128)S(1)}, f32[5,32,128]{2,1,0:T(8,128)S(1)}, f32[5,32,128]{2,1,0:T(8,128)S(1)}, f32[5,32,128]{2,1,0:T(...) fusion(f32[32,128]{1,0:T(8,128)} %get-tuple-element.775, ...), kind=kLoop, calls=%fused_computation.674 | loop fusion | flops 7987200 | bytes 19021824 | tf_op jit(solution)/shard_map/sub | solution.py:68
  149.0 4.5 %constant_dynamic-update-slice_fusion.127 = (f32[5,128,32,128]{3,2,0,1:T(8,128)S(1)}, f32[5,32,128]{2,1,0:T(8,128)S(1)}, f32[5,32,128]{2,1,0:T(8,128)S(1)}, f32[...) fusion(f32[32,128]{1,0:T(8,128)} %get-tuple-element.915, ...), kind=kLoop, calls=%fused_computation.189 | loop fusion | flops 7106559 | bytes 15630336
  154.9 0.7 constant_dynamic-update-slice_fusion.125
  155.7 0.7 constant_dynamic-update-slice_fusion.123
  156.4 0.7 constant_dynamic-update-slice_fusion.121
  157.2 0.7 constant_dynamic-update-slice_fusion.119
  158.0 0.7 constant_dynamic-update-slice_fusion.117
  158.7 0.7 constant_dynamic-update-slice_fusion.115
  159.5 0.7 constant_dynamic-update-slice_fusion.113
  160.3 0.7 constant_dynamic-update-slice_fusion.111
  161.0 0.7 constant_dynamic-update-slice_fusion.109
  161.8 0.7 constant_dynamic-update-slice_fusion.107
  162.6 0.7 constant_dynamic-update-slice_fusion.105
  163.3 0.7 constant_dynamic-update-slice_fusion.103
  164.1 0.7 constant_dynamic-update-slice_fusion.101
  164.9 0.7 constant_dynamic-update-slice_fusion.99
  165.6 0.7 constant_dynamic-update-slice_fusion.97
  166.4 0.7 constant_dynamic-update-slice_fusion.95
  172.2 3.9 %copy-done.2 = f32[5,128,32,128]{3,2,0,1:T(8,128)} copy-done((f32[5,128,32,128]{3,2,0,1:T(8,128)}, f32[5,128,32,128]{3,2,0,1:T(8,128)S(1)}, u32[]{:S(2)}) %copy-start.2) | copy-done | bytes 10485784
  176.1 1.8 slice_bitcast_fusion.1
  177.9 13.1 %all-gather.1 = f32[24,32,128]{2,1,0:T(8,128)S(1)} all-gather(f32[3,32,128]{2,1,0:T(8,128)S(1)} %slice.2111), channel_id=3, replica_groups=mesh['wn'=8,'xz'=16] {'wn'}, dimensions={0}, use_global_device_ids=true | all-gather | bytes 442368 | tf_op jit(solution)/shard_map/all_gather | solution.py:31
  191.0 12.7 %all_gather.26 = f32[8,32,128]{2,1,0:T(8,128)S(1)} all-gather(f32[1,32,128]{2,1,0:T(8,128)S(1)} %get-tuple-element.1077), channel_id=1, replica_groups=mesh['wn'=8,'xz'=16] {'wn'}, dimensions={0}, use_global_device_ids=true | all-gather | bytes 147456 | tf_op jit(solution)/shard_map/all_gather | solution.py:31
  203.7 12.7 %all_gather.27 = f32[8,32,128]{2,1,0:T(8,128)S(1)} all-gather(f32[1,32,128]{2,1,0:T(8,128)S(1)} %get-tuple-element.1076), channel_id=1, replica_groups=mesh['wn'=8,'xz'=16] {'wn'}, dimensions={0}, use_global_device_ids=true | all-gather | bytes 147456 | tf_op jit(solution)/shard_map/all_gather | solution.py:31
  216.4 13.0 %all-gather = f32[24,32,128]{2,1,0:T(8,128)S(1)} all-gather(f32[3,32,128]{2,1,0:T(8,128)S(1)} %slice.2110), channel_id=2, replica_groups=mesh['wn'=8,'xz'=16] {'wn'}, dimensions={0}, use_global_device_ids=true | all-gather | bytes 442368 | tf_op jit(solution)/shard_map/all_gather | solution.py:31
  229.4 13.8 %all_gather.24 = f32[8,32,128]{2,1,0:T(8,128)} all-gather(f32[1,32,128]{2,1,0:T(8,128)S(1)} %get-tuple-element.1081), channel_id=1, replica_groups=mesh['wn'=8,'xz'=16] {'wn'}, dimensions={0}, use_global_device_ids=true | all-gather | bytes 147456 | tf_op jit(solution)/shard_map/all_gather | solution.py:31
  243.2 12.7 %all_gather.25 = f32[8,32,128]{2,1,0:T(8,128)S(1)} all-gather(f32[1,32,128]{2,1,0:T(8,128)S(1)} %get-tuple-element.1080), channel_id=1, replica_groups=mesh['wn'=8,'xz'=16] {'wn'}, dimensions={0}, use_global_device_ids=true | all-gather | bytes 147456 | tf_op jit(solution)/shard_map/all_gather | solution.py:31
  255.9 6.8 %while.34 = (s32[]{:T(128)}, f32[32,128]{1,0:T(8,128)S(1)}, f32[3,32,128]{2,1,0:T(8,128)S(1)}, s32[]{:T(128)}, f32[8,32,128]{2,1,0:T(8,128)}, /*index=5*/f32[8,3...) while((s32[]{:T(128)}, f32[32,128]{1,0:T(8,128)S(1)}, ...), condition=%wide.region_1.2_spmd.clone, body=%wide.region_0.1_spmd.clone.sunk | while | flops 126980 | bytes 442523 | solution.py:42
  256.2 0.7 fusion.527
  257.0 0.7 fusion.527
  257.9 0.7 fusion.527
  258.7 0.7 fusion.527
  259.5 0.7 fusion.527
  260.4 0.7 fusion.527
  261.2 0.7 fusion.527
  262.0 0.7 fusion.527
  262.8 6.5 %while.35 = (s32[]{:T(128)}, f32[32,128]{1,0:T(8,128)S(1)}, f32[3,32,128]{2,1,0:T(8,128)S(1)}, s32[]{:T(128)}, f32[8,32,128]{2,1,0:T(8,128)S(1)}, /*index=5*/f32...) while((s32[]{:T(128)}, f32[32,128]{1,0:T(8,128)S(1)}, ...), condition=%wide.region_3.4_spmd.clone, body=%wide.region_2.3_spmd.clone.sunk | while | flops 151560 | bytes 475353 | solution.py:42
  269.3 0.8 multiply_subtract_fusion.128
  270.0 0.9 multiply_add_fusion.1
  270.9 5.8 %fusion.20 = f32[3,128,32,128]{3,2,0,1:T(8,128)S(1)} fusion(f32[5,128,32,128]{3,2,0,1:T(8,128)} %copy-done.2, f32[3,32,128]{2,1,0:T(8,128)S(1)} %get-tuple-element.1073, f32[128,32,128]{2,1,0:T(8,128)} %get-tuple-element.903, f32[3,32,128]{2,1,0:T(8,128)S(1)} %get-tuple-element.1072, f32[128,32,128]{2,1,0:T(8,128)S(1)} %get-tuple-element.902), kind=kLoop, calls=%fused_computation.33 | loop fusion | flops 6291456 | bytes 16875520 | tf_op jit(solution)/shard_map/add | solution.py:111
  276.8 3.4 %copy.388 = f32[3,128,32,128]{3,2,1,0:T(8,128)} copy(f32[3,128,32,128]{3,2,0,1:T(8,128)S(1)} %fusion.20) | data formatting | bytes 12582912 | tf_op jit(solution)/shard_map/add | solution.py:111
  (461 shorter events, 27.7 us)
Async XLA Ops:
  1.7 59.6 %collective-permute-start = (f32[4,1,32,128]{3,2,1,0:T(8,128)}, f32[4,1,32,128]{3,2,1,0:T(8,128)}, u32[]{:S(2)}, u32[]{:S(2)}) collective-permute-start(f32[4,1,32,128]{3,2,1,0:T(8,128)} %get-tuple-element.904), channel_id=1, source_target_pairs={{16,0},{32,16},{48,32},{64,48},{80,64},{96,80},{112,96},{17,1},{33... | collective-permute-start | bytes 196616 | tf_op jit(solution)/shard_map/ppermute | solution.py:22
  5.1 56.2 %collective-permute-start.1 = (f32[4,1,32,128]{3,2,1,0:T(8,128)}, f32[4,1,32,128]{3,2,1,0:T(8,128)}, u32[]{:S(2)}, u32[]{:S(2)}) collective-permute-start(f32[4,1,32,128]{3,2,1,0:T(8,128)} %get-tuple-element.905), channel_id=1, source_target_pairs={{0,16},{16,32},{32,48},{48,64},{64,80},{80,96},{96,112},{1,17},{17... | collective-permute-start | bytes 196616 | tf_op jit(solution)/shard_map/ppermute | solution.py:20
  21.2 26.5 %collective-permute-start.2 = (f32[3,128,32,1]{1,2,3,0:T(8,128)}, f32[3,128,32,1]{1,2,3,0:T(8,128)}, u32[]{:S(2)}, u32[]{:S(2)}) collective-permute-start(f32[3,128,32,1]{1,2,3,0:T(8,128)} %copy.389), channel_id=1, source_target_pairs={{1,0},{2,1},{3,2},{4,3},{5,4},{6,5},{7,6},{8,7},{9,8},{10,9},{11,1... | collective-permute-start | bytes 147464 | tf_op jit(solution)/shard_map/ppermute | solution.py:22
  33.3 21.3 %collective-permute-start.3 = (f32[3,128,32,1]{1,2,3,0:T(8,128)}, f32[3,128,32,1]{1,2,3,0:T(8,128)}, u32[]{:S(2)}, u32[]{:S(2)}) collective-permute-start(f32[3,128,32,1]{1,2,3,0:T(8,128)} %copy.390), channel_id=1, source_target_pairs={{0,1},{1,2},{2,3},{3,4},{4,5},{5,6},{6,7},{7,8},{8,9},{9,10},{10,1... | collective-permute-start | bytes 147464 | tf_op jit(solution)/shard_map/ppermute | solution.py:20
  66.4 55.3 %copy-start.95 = (f32[32,128]{1,0:T(8,128)}, f32[32,128]{1,0:T(8,128)S(1)}, u32[]{:S(2)}) copy-start(f32[32,128]{1,0:T(8,128)S(1)} %get-tuple-element.1043) | copy-start | bytes 49156
  66.4 55.3 %copy-start.96 = (f32[32,128]{1,0:T(8,128)}, f32[32,128]{1,0:T(8,128)S(1)}, u32[]{:S(2)}) copy-start(f32[32,128]{1,0:T(8,128)S(1)} %get-tuple-element.1045) | copy-start | bytes 49156
  68.6 47.3 %copy-start.10 = (f32[32,128]{1,0:T(8,128)}, f32[32,128]{1,0:T(8,128)S(1)}, u32[]{:S(2)}) copy-start(f32[32,128]{1,0:T(8,128)S(1)} %get-tuple-element.816) | copy-start | bytes 49156
  75.5 46.3 %copy-start.4 = (f32[1,32,128]{2,1,0:T(8,128)}, f32[1,32,128]{2,1,0:T(8,128)S(1)}, u32[]{:S(2)}) copy-start(f32[1,32,128]{2,1,0:T(8,128)S(1)} %get-tuple-element.606) | copy-start | bytes 49156
  76.1 45.6 %copy-start.6 = (f32[1,32,128]{2,1,0:T(8,128)}, f32[1,32,128]{2,1,0:T(8,128)S(1)}, u32[]{:S(2)}) copy-start(f32[1,32,128]{2,1,0:T(8,128)S(1)} %get-tuple-element.609) | copy-start | bytes 49156
  76.7 45.0 %copy-start.8 = (f32[1,32,128]{2,1,0:T(8,128)}, f32[1,32,128]{2,1,0:T(8,128)S(1)}, u32[]{:S(2)}) copy-start(f32[1,32,128]{2,1,0:T(8,128)S(1)} %get-tuple-element.612) | copy-start | bytes 49156
  77.4 38.5 %copy-start.13 = (f32[1,32,128]{2,1,0:T(8,128)}, f32[1,32,128]{2,1,0:T(8,128)S(1)}, u32[]{:S(2)}) copy-start(f32[1,32,128]{2,1,0:T(8,128)S(1)} %get-tuple-element.615) | copy-start | bytes 49156
  77.4 38.5 %copy-start.105 = (f32[1,32,128]{2,1,0:T(8,128)}, f32[1,32,128]{2,1,0:T(8,128)S(1)}, u32[]{:S(2)}) copy-start(f32[1,32,128]{2,1,0:T(8,128)S(1)} %get-tuple-element.614) | copy-start | bytes 49156
  77.4 44.3 %copy-start.97 = (f32[32,128]{1,0:T(8,128)}, f32[32,128]{1,0:T(8,128)S(1)}, u32[]{:S(2)}) copy-start(f32[32,128]{1,0:T(8,128)S(1)} %get-tuple-element.1055) | copy-start | bytes 49156
  77.4 44.3 %copy-start.98 = (f32[32,128]{1,0:T(8,128)}, f32[32,128]{1,0:T(8,128)S(1)}, u32[]{:S(2)}) copy-start(f32[32,128]{1,0:T(8,128)S(1)} %get-tuple-element.1057) | copy-start | bytes 49156
  77.4 44.3 %copy-start.99 = (f32[32,128]{1,0:T(8,128)}, f32[32,128]{1,0:T(8,128)S(1)}, u32[]{:S(2)}) copy-start(f32[32,128]{1,0:T(8,128)S(1)} %get-tuple-element.1059) | copy-start | bytes 49156
  77.4 44.3 %copy-start.100 = (f32[32,128]{1,0:T(8,128)}, f32[32,128]{1,0:T(8,128)S(1)}, u32[]{:S(2)}) copy-start(f32[32,128]{1,0:T(8,128)S(1)} %get-tuple-element.1061) | copy-start | bytes 49156
  77.4 44.3 %copy-start.101 = (f32[32,128]{1,0:T(8,128)}, f32[32,128]{1,0:T(8,128)S(1)}, u32[]{:S(2)}) copy-start(f32[32,128]{1,0:T(8,128)S(1)} %get-tuple-element.1063) | copy-start | bytes 49156
  77.5 44.3 %copy-start.102 = (f32[32,128]{1,0:T(8,128)}, f32[32,128]{1,0:T(8,128)S(1)}, u32[]{:S(2)}) copy-start(f32[32,128]{1,0:T(8,128)S(1)} %get-tuple-element.1065) | copy-start | bytes 49156
  77.5 44.3 %copy-start.103 = (f32[32,128]{1,0:T(8,128)}, f32[32,128]{1,0:T(8,128)S(1)}, u32[]{:S(2)}) copy-start(f32[32,128]{1,0:T(8,128)S(1)} %get-tuple-element.1066) | copy-start | bytes 49156
  78.1 37.8 %copy-start.16 = (f32[1,32,128]{2,1,0:T(8,128)}, f32[1,32,128]{2,1,0:T(8,128)S(1)}, u32[]{:S(2)}) copy-start(f32[1,32,128]{2,1,0:T(8,128)S(1)} %get-tuple-element.618) | copy-start | bytes 49156
  78.7 37.2 %copy-start.19 = (f32[1,32,128]{2,1,0:T(8,128)}, f32[1,32,128]{2,1,0:T(8,128)S(1)}, u32[]{:S(2)}) copy-start(f32[1,32,128]{2,1,0:T(8,128)S(1)} %get-tuple-element.621) | copy-start | bytes 49156
  79.4 36.6 %copy-start.25 = (f32[1,32,128]{2,1,0:T(8,128)}, f32[1,32,128]{2,1,0:T(8,128)S(1)}, u32[]{:S(2)}) copy-start(f32[1,32,128]{2,1,0:T(8,128)S(1)} %get-tuple-element.624) | copy-start | bytes 49156
  79.4 36.6 %copy-start.108 = (f32[1,32,128]{2,1,0:T(8,128)}, f32[1,32,128]{2,1,0:T(8,128)S(1)}, u32[]{:S(2)}) copy-start(f32[1,32,128]{2,1,0:T(8,128)S(1)} %get-tuple-element.623) | copy-start | bytes 49156
  80.0 35.9 %copy-start.28 = (f32[1,32,128]{2,1,0:T(8,128)}, f32[1,32,128]{2,1,0:T(8,128)S(1)}, u32[]{:S(2)}) copy-start(f32[1,32,128]{2,1,0:T(8,128)S(1)} %get-tuple-element.627) | copy-start | bytes 49156
  80.0 35.9 %copy-start.109 = (f32[1,32,128]{2,1,0:T(8,128)}, f32[1,32,128]{2,1,0:T(8,128)S(1)}, u32[]{:S(2)}) copy-start(f32[1,32,128]{2,1,0:T(8,128)S(1)} %get-tuple-element.626) | copy-start | bytes 49156
  80.6 35.3 %copy-start.31 = (f32[1,32,128]{2,1,0:T(8,128)}, f32[1,32,128]{2,1,0:T(8,128)S(1)}, u32[]{:S(2)}) copy-start(f32[1,32,128]{2,1,0:T(8,128)S(1)} %get-tuple-element.630) | copy-start | bytes 49156
  80.6 35.3 %copy-start.110 = (f32[1,32,128]{2,1,0:T(8,128)}, f32[1,32,128]{2,1,0:T(8,128)S(1)}, u32[]{:S(2)}) copy-start(f32[1,32,128]{2,1,0:T(8,128)S(1)} %get-tuple-element.629) | copy-start | bytes 49156
  81.3 34.7 %copy-start.34 = (f32[1,32,128]{2,1,0:T(8,128)}, f32[1,32,128]{2,1,0:T(8,128)S(1)}, u32[]{:S(2)}) copy-start(f32[1,32,128]{2,1,0:T(8,128)S(1)} %get-tuple-element.633) | copy-start | bytes 49156
  81.3 34.7 %copy-start.111 = (f32[1,32,128]{2,1,0:T(8,128)}, f32[1,32,128]{2,1,0:T(8,128)S(1)}, u32[]{:S(2)}) copy-start(f32[1,32,128]{2,1,0:T(8,128)S(1)} %get-tuple-element.632) | copy-start | bytes 49156
  81.9 34.1 %copy-start.37 = (f32[1,32,128]{2,1,0:T(8,128)}, f32[1,32,128]{2,1,0:T(8,128)S(1)}, u32[]{:S(2)}) copy-start(f32[1,32,128]{2,1,0:T(8,128)S(1)} %get-tuple-element.636) | copy-start | bytes 49156
  81.9 34.1 %copy-start.112 = (f32[1,32,128]{2,1,0:T(8,128)}, f32[1,32,128]{2,1,0:T(8,128)S(1)}, u32[]{:S(2)}) copy-start(f32[1,32,128]{2,1,0:T(8,128)S(1)} %get-tuple-element.635) | copy-start | bytes 49156
  82.5 33.5 %copy-start.40 = (f32[1,32,128]{2,1,0:T(8,128)}, f32[1,32,128]{2,1,0:T(8,128)S(1)}, u32[]{:S(2)}) copy-start(f32[1,32,128]{2,1,0:T(8,128)S(1)} %get-tuple-element.639) | copy-start | bytes 49156
  83.2 32.9 %copy-start.43 = (f32[1,32,128]{2,1,0:T(8,128)}, f32[1,32,128]{2,1,0:T(8,128)S(1)}, u32[]{:S(2)}) copy-start(f32[1,32,128]{2,1,0:T(8,128)S(1)} %get-tuple-element.642) | copy-start | bytes 49156
  83.8 32.2 %copy-start.46 = (f32[1,32,128]{2,1,0:T(8,128)}, f32[1,32,128]{2,1,0:T(8,128)S(1)}, u32[]{:S(2)}) copy-start(f32[1,32,128]{2,1,0:T(8,128)S(1)} %get-tuple-element.645) | copy-start | bytes 49156
  84.5 31.6 %copy-start.22 = (f32[1,32,128]{2,1,0:T(8,128)}, f32[1,32,128]{2,1,0:T(8,128)S(1)}, u32[]{:S(2)}) copy-start(f32[1,32,128]{2,1,0:T(8,128)S(1)} %get-tuple-element.648) | copy-start | bytes 49156
  84.5 31.6 %copy-start.115 = (f32[1,32,128]{2,1,0:T(8,128)}, f32[1,32,128]{2,1,0:T(8,128)S(1)}, u32[]{:S(2)}) copy-start(f32[1,32,128]{2,1,0:T(8,128)S(1)} %get-tuple-element.647) | copy-start | bytes 49156
  85.2 30.9 %copy-start.49 = (f32[1,32,128]{2,1,0:T(8,128)}, f32[1,32,128]{2,1,0:T(8,128)S(1)}, u32[]{:S(2)}) copy-start(f32[1,32,128]{2,1,0:T(8,128)S(1)} %get-tuple-element.891) | copy-start | bytes 49156
  85.2 36.7 %copy-start.104 = (f32[32,128]{1,0:T(8,128)}, f32[32,128]{1,0:T(8,128)S(1)}, u32[]{:S(2)}) copy-start(f32[32,128]{1,0:T(8,128)S(1)} %get-tuple-element.916) | copy-start | bytes 49156
  122.1 26.5 %copy-start.5 = (f32[1,32,128]{2,1,0:T(8,128)S(1)}, f32[1,32,128]{2,1,0:T(8,128)}, u32[]{:S(2)}) copy-start(f32[1,32,128]{2,1,0:T(8,128)} %copy-done.4) | copy-start | bytes 49156
  122.1 26.5 %copy-start.7 = (f32[1,32,128]{2,1,0:T(8,128)S(1)}, f32[1,32,128]{2,1,0:T(8,128)}, u32[]{:S(2)}) copy-start(f32[1,32,128]{2,1,0:T(8,128)} %copy-done.6) | copy-start | bytes 49156
  122.1 26.5 %copy-start.9 = (f32[1,32,128]{2,1,0:T(8,128)S(1)}, f32[1,32,128]{2,1,0:T(8,128)}, u32[]{:S(2)}) copy-start(f32[1,32,128]{2,1,0:T(8,128)} %copy-done.8) | copy-start | bytes 49156
  122.2 26.5 %copy-start.12 = (f32[32,128]{1,0:T(8,128)S(1)}, f32[32,128]{1,0:T(8,128)}, u32[]{:S(2)}) copy-start(f32[32,128]{1,0:T(8,128)} %copy-done.10) | copy-start | bytes 49156
  122.2 26.5 %copy-start.15 = (f32[1,32,128]{2,1,0:T(8,128)S(1)}, f32[1,32,128]{2,1,0:T(8,128)}, u32[]{:S(2)}) copy-start(f32[1,32,128]{2,1,0:T(8,128)} %copy-done.13) | copy-start | bytes 49156
  122.2 26.5 %copy-start.18 = (f32[1,32,128]{2,1,0:T(8,128)S(1)}, f32[1,32,128]{2,1,0:T(8,128)}, u32[]{:S(2)}) copy-start(f32[1,32,128]{2,1,0:T(8,128)} %copy-done.16) | copy-start | bytes 49156
  122.2 26.5 %copy-start.21 = (f32[1,32,128]{2,1,0:T(8,128)S(1)}, f32[1,32,128]{2,1,0:T(8,128)}, u32[]{:S(2)}) copy-start(f32[1,32,128]{2,1,0:T(8,128)} %copy-done.19) | copy-start | bytes 49156
  122.2 26.5 %copy-start.24 = (f32[1,32,128]{2,1,0:T(8,128)S(1)}, f32[1,32,128]{2,1,0:T(8,128)}, u32[]{:S(2)}) copy-start(f32[1,32,128]{2,1,0:T(8,128)} %copy-done.22) | copy-start | bytes 49156
  122.2 26.5 %copy-start.27 = (f32[1,32,128]{2,1,0:T(8,128)S(1)}, f32[1,32,128]{2,1,0:T(8,128)}, u32[]{:S(2)}) copy-start(f32[1,32,128]{2,1,0:T(8,128)} %copy-done.25) | copy-start | bytes 49156
  122.2 26.5 %copy-start.30 = (f32[1,32,128]{2,1,0:T(8,128)S(1)}, f32[1,32,128]{2,1,0:T(8,128)}, u32[]{:S(2)}) copy-start(f32[1,32,128]{2,1,0:T(8,128)} %copy-done.28) | copy-start | bytes 49156
  122.2 26.5 %copy-start.33 = (f32[1,32,128]{2,1,0:T(8,128)S(1)}, f32[1,32,128]{2,1,0:T(8,128)}, u32[]{:S(2)}) copy-start(f32[1,32,128]{2,1,0:T(8,128)} %copy-done.31) | copy-start | bytes 49156
  122.2 26.5 %copy-start.36 = (f32[1,32,128]{2,1,0:T(8,128)S(1)}, f32[1,32,128]{2,1,0:T(8,128)}, u32[]{:S(2)}) copy-start(f32[1,32,128]{2,1,0:T(8,128)} %copy-done.34) | copy-start | bytes 49156
  122.2 26.5 %copy-start.39 = (f32[1,32,128]{2,1,0:T(8,128)S(1)}, f32[1,32,128]{2,1,0:T(8,128)}, u32[]{:S(2)}) copy-start(f32[1,32,128]{2,1,0:T(8,128)} %copy-done.37) | copy-start | bytes 49156
  122.3 26.5 %copy-start.42 = (f32[1,32,128]{2,1,0:T(8,128)S(1)}, f32[1,32,128]{2,1,0:T(8,128)}, u32[]{:S(2)}) copy-start(f32[1,32,128]{2,1,0:T(8,128)} %copy-done.40) | copy-start | bytes 49156
  122.3 26.5 %copy-start.45 = (f32[1,32,128]{2,1,0:T(8,128)S(1)}, f32[1,32,128]{2,1,0:T(8,128)}, u32[]{:S(2)}) copy-start(f32[1,32,128]{2,1,0:T(8,128)} %copy-done.43) | copy-start | bytes 49156
  122.3 26.5 %copy-start.48 = (f32[1,32,128]{2,1,0:T(8,128)S(1)}, f32[1,32,128]{2,1,0:T(8,128)}, u32[]{:S(2)}) copy-start(f32[1,32,128]{2,1,0:T(8,128)} %copy-done.46) | copy-start | bytes 49156
  122.3 26.5 %copy-start.51 = (f32[1,32,128]{2,1,0:T(8,128)S(1)}, f32[1,32,128]{2,1,0:T(8,128)}, u32[]{:S(2)}) copy-start(f32[1,32,128]{2,1,0:T(8,128)} %copy-done.49) | copy-start | bytes 49156
  122.3 26.5 %copy-start.52 = (f32[32,128]{1,0:T(8,128)S(1)}, f32[32,128]{1,0:T(8,128)}, u32[]{:S(2)}) copy-start(f32[32,128]{1,0:T(8,128)} %get-tuple-element.817) | copy-start | bytes 49156
  122.3 26.5 %copy-start.53 = (f32[32,128]{1,0:T(8,128)S(1)}, f32[32,128]{1,0:T(8,128)}, u32[]{:S(2)}) copy-start(f32[32,128]{1,0:T(8,128)} %get-tuple-element.821) | copy-start | bytes 49156
  122.3 26.5 %copy-start.54 = (f32[32,128]{1,0:T(8,128)S(1)}, f32[32,128]{1,0:T(8,128)}, u32[]{:S(2)}) copy-start(f32[32,128]{1,0:T(8,128)} %get-tuple-element.825) | copy-start | bytes 49156
  122.3 26.5 %copy-start.55 = (f32[32,128]{1,0:T(8,128)S(1)}, f32[32,128]{1,0:T(8,128)}, u32[]{:S(2)}) copy-start(f32[32,128]{1,0:T(8,128)} %get-tuple-element.829) | copy-start | bytes 49156
  122.3 26.5 %copy-start.56 = (f32[32,128]{1,0:T(8,128)S(1)}, f32[32,128]{1,0:T(8,128)}, u32[]{:S(2)}) copy-start(f32[32,128]{1,0:T(8,128)} %get-tuple-element.833) | copy-start | bytes 49156
  122.3 26.5 %copy-start.57 = (f32[32,128]{1,0:T(8,128)S(1)}, f32[32,128]{1,0:T(8,128)}, u32[]{:S(2)}) copy-start(f32[32,128]{1,0:T(8,128)} %get-tuple-element.837) | copy-start | bytes 49156
  122.4 26.5 %copy-start.58 = (f32[32,128]{1,0:T(8,128)S(1)}, f32[32,128]{1,0:T(8,128)}, u32[]{:S(2)}) copy-start(f32[32,128]{1,0:T(8,128)} %get-tuple-element.841) | copy-start | bytes 49156
  122.4 26.5 %copy-start.59 = (f32[32,128]{1,0:T(8,128)S(1)}, f32[32,128]{1,0:T(8,128)}, u32[]{:S(2)}) copy-start(f32[32,128]{1,0:T(8,128)} %get-tuple-element.845) | copy-start | bytes 49156
  122.4 26.5 %copy-start.60 = (f32[32,128]{1,0:T(8,128)S(1)}, f32[32,128]{1,0:T(8,128)}, u32[]{:S(2)}) copy-start(f32[32,128]{1,0:T(8,128)} %get-tuple-element.849) | copy-start | bytes 49156
  (68 other events, 784.2 us)
where the time goes:
time: 284 us; the launch traced here: 280 us
  other arithmetic  124 us (44%)
  blocking collectives  78 us (27%)
  local copies, waits for them, and re-layouts  61.5 us (22%)
  starting transfers between devices  12.8 us (5%)
    all_gather x6, blocking collectives, entering(): everything = jax.tree.map(lambda part: lax.all_gather(part, axis), x)  78 us
    sub x1, other arithmetic, advect(): velocity - (x_courant * velocity[0] * diff_x + y_courant * velocity[1] *...  27 us
    sub x1, other arithmetic, thomas_rows(): following = saved[position][1] - saved[position][0] * following  26.1 us
    unnamed x69, other arithmetic  20 us
    unnamed x321, local copies, waits for them, and re-layouts  16.8 us
    mul x22, other arithmetic, thomas_rows(): following = saved[position][1] - saved[position][0] * following  14.7 us
    ppermute x2, starting transfers between devices, extended(): lax.ppermute(head, axis, [((i + 1) % count, i) for i in range(ends)])  9.66 us
    slice x1, local copies, waits for them, and re-layouts, extended(): head = lax.slice_in_dim(cells, 0, width, axis=dim)  7.02 us
  transfers between devices with their start and end apart: 4, of which 0 were waited for; matrix products, arithmetic and copies ran while one was open for 17% of the time, Pallas kernels for 0%

commit v1 on v0

v1 whole, which is shorter than its diff:
```python
import functools

import jax
import jax.numpy as jnp
from jax import lax
from jax.experimental import pallas as pl
from jax.experimental.pallas import tpu as pltpu
from jax.sharding import PartitionSpec as P

x_courant = 0.25
y_courant = 0.5
z_courant = 0.25
face_rate = 1000.0

SUB = 8
LANES = 128
VMEM = pltpu.VMEM
f32 = jnp.float32
bf16 = jnp.bfloat16


def lane_index():
    return lax.broadcasted_iota(jnp.int32, (SUB, LANES), 1)


def sub_index():
    return lax.broadcasted_iota(jnp.int32, (SUB, LANES), 0)


def tile(ref, *lead, t):
    return ref[(*lead, pl.ds(t * SUB, SUB), slice(None))]


def put(ref, value, *lead, t):
    ref[(*lead, pl.ds(t * SUB, SUB), slice(None))] = value


def square(ref, *lead, start, nx):
    rows = LANES // nx
    return ref[(*lead, pl.ds(start, rows))].reshape(LANES, LANES)


def head_kernel(
    chunk, vel_hbm, visc_hbm, marks, vel, low, high, row_out, row_in, wid, hid, rec, fwd, flags, visc, sems
):
    comps, rows, nx, _ = vel_hbm.shape
    tiles = nx // SUB
    group = LANES // nx
    chunks = rows // chunk

    def visc_copy(k):
        span = pl.ds(k * chunk, chunk)
        return pltpu.make_async_copy(visc_hbm.at[span], visc.at[span], sems.at[0, k])

    def vel_copy(k):
        span = pl.ds(k * chunk, chunk)
        inner = pl.ds(k * chunk + 1, chunk)
        return pltpu.make_async_copy(vel_hbm.at[:, span], vel.at[:, inner], sems.at[1, k])

    for k in range(chunks):
        visc_copy(k).start()
    for k in range(chunks):
        vel_copy(k).start()
    flags[...] = marks[...]
    zero = jnp.zeros((SUB, LANES), f32)
    for c in range(comps):
        for t in range(tiles):
            put(vel, zero, c, 0, t=t)
            put(vel, zero, c, rows + 1, t=t)
    wall_low = jnp.broadcast_to(marks[1:2, :], (SUB, LANES))
    wall_high = jnp.broadcast_to(marks[2:3, :], (SUB, LANES))

    def body(k, state, last=False):
        if not last:
            visc_copy(k + 1).wait()
        vel_copy(k).wait()
        state = list(state)
        for r in range(chunk):
            y = k * chunk + r
            end = last and r == chunk - 1
            for t in range(tiles):
                extra, cell, face, reach = state[4 * t : 4 * t + 4]
                inner = 1.0 + extra
                if end:
                    next_cell = cell
                    next_face = wall_high * (2.0 * cell)
                else:
                    next_cell = face_rate * tile(visc, y + 1, t=t)
                    next_face = cell + next_cell
                r_ = pltpu.reciprocal(inner + next_face, approx=False)
                w = r_ if end else next_face * r_
                h = face * r_
                reach = h * reach
                put(wid, w, y, t=t)
                put(hid, h, y, t=t)
                put(rec, r_, y, t=t)
                put(fwd, reach, y, t=t)
                state[4 * t : 4 * t + 4] = [w * inner, next_cell, next_face, reach]
            if r % group == group - 1:
                start = k * chunk + r - group + 1
                spot = (k * chunk + r) // group
                for c in range(comps):
                    turned = square(vel, c, start=start + 1, nx=nx).T
                    low[c, pl.ds(spot, 1), :] = turned[:1]
                    high[c, pl.ds(spot, 1), :] = turned[LANES - 1 :]
        return tuple(state)

    visc_copy(0).wait()
    state = []
    one = jnp.ones((SUB, LANES), f32)
    for t in range(tiles):
        cell = face_rate * tile(visc, 0, t=t)
        state += [wall_low * (2.0 * cell), cell, one, one]
    state = lax.fori_loop(0, chunks - 1, body, tuple(state))
    body(chunks - 1, state, last=True)

    upper = jnp.broadcast_to(marks[0:1, :], (SUB, LANES)) > 0.5
    for c in range(comps + 1):
        for t in range(tiles):
            if c < comps:
                first, end = tile(vel, c, 1, t=t), tile(vel, c, rows, t=t)
            else:
                first, end = tile(visc, 0, t=t), tile(visc, rows - 1, t=t)
            put(row_out, jnp.where(upper, end, first), c, t=t)
            put(row_in, jnp.where(upper, first, end), c, t=t)


def shifted(ref, lead, t, tiles, forward, sub):
    if forward:
        if t < tiles - 1:
            return ref[(*lead, pl.ds(t * SUB + 1, SUB), slice(None))]
        mixed = jnp.where(sub == 0, tile(ref, *lead, t=0), tile(ref, *lead, t=t))
        return pltpu.roll(mixed, SUB - 1, 0)
    if t > 0:
        return ref[(*lead, pl.ds(t * SUB - 1, SUB), slice(None))]
    mixed = jnp.where(sub == SUB - 1, tile(ref, *lead, t=tiles - 1), tile(ref, *lead, t=t))
    return pltpu.roll(mixed, 1, 0)


def block_kernel(vel, wid, rec, fwd, rhs, left, right, ends, dots, edges, buf_a, buf_b):
    comps, rows, nx, _ = rhs.shape
    tiles = nx // SUB
    group = LANES // nx
    groups = rows // group
    sub = sub_index()
    a = lax.broadcasted_iota(jnp.int32, (2 * LANES, LANES), 0) % LANES
    b = lax.broadcasted_iota(jnp.int32, (2 * LANES, LANES), 1)
    ahead = (a == (b + 1) % LANES).astype(f32)
    behind = (a == (b + LANES - 1) % LANES).astype(f32)
    central = (z_courant * (ahead - behind)).astype(bf16)

    def differ(buf, g):
        for c in range(comps):
            whole = square(vel, c, start=g * group + 1, nx=nx)
            coarse = whole.astype(bf16)
            fine = (whole - coarse.astype(f32)).astype(bf16)
            buf[c] = jnp.dot(jnp.concatenate([coarse, fine], 1), central, preferred_element_type=f32)

    def process(g, buf, state):
        state = list(state)
        for r in reversed(range(group)):
            y = g * group + r
            for t in range(tiles):
                ul, ur, *sums = state[8 * t : 8 * t + 8]
                w = tile(wid, y, t=t)
                ul, ur = tile(fwd, y, t=t) + w * ul, w * ur
                put(left, ul, y, t=t)
                put(right, ur, y, t=t)
                mid = [tile(vel, c, y + 1, t=t) for c in range(comps)]
                rate_x, rate_y = x_courant * mid[0], y_courant * mid[1]
                for c in range(comps):
                    lead = (c, y + 1)
                    diff_x = shifted(vel, lead, t, tiles, True, sub) - shifted(vel, lead, t, tiles, False, sub)
                    diff_y = tile(vel, c, y + 2, t=t) - tile(vel, c, y, t=t)
                    diff_z = buf[c, pl.ds(r * nx + t * SUB, SUB), :]
                    source = mid[c] - (rate_x * diff_x + rate_y * diff_y + mid[2] * diff_z)
                    put(rhs, source, c, y, t=t)
                    sums[c] = sums[c] + ul * source
                    sums[comps + c] = sums[comps + c] + ur * source
                state[8 * t : 8 * t + 8] = [ul, ur, *sums]
        return tuple(state)

    def pack(g):
        for k, ref in enumerate((left, right)):
            turned = square(ref, start=g * group, nx=nx).T
            edges[2 * k, pl.ds(g, 1), :] = turned[:1]
            edges[2 * k + 1, pl.ds(g, 1), :] = turned[LANES - 1 :]

    def body(m, state):
        g = groups - 1 - 2 * m
        differ(buf_b, g - 1)
        state = process(g, buf_a, state)
        pack(jnp.minimum(g + 1, groups - 1))
        differ(buf_a, jnp.maximum(g - 2, 0))
        state = process(g - 1, buf_b, state)
        pack(g)
        return state

    zero, one = jnp.zeros((SUB, LANES), f32), jnp.ones((SUB, LANES), f32)
    differ(buf_a, groups - 1)
    state = ([zero, one] + [zero] * 6) * tiles
    state = lax.fori_loop(0, groups // 2, body, tuple(state))
    pack(0)
    for t in range(tiles):
        ul, ur, *sums = state[8 * t : 8 * t + 8]
        put(ends, ul, 0, t=t)
        put(ends, tile(fwd, rows - 1, t=t), 1, t=t)
        put(ends, tile(rec, rows - 1, t=t), 2, t=t)
        for k in range(6):
            put(dots, sums[k], k, t=t)


def edge_kernel(low, high, from_left, from_right, edges, dots, edge_low, edge_high, values):
    comps, groups, _ = low.shape
    _, nx, _ = dots.shape
    lane, sub = lane_index(), sub_index()
    edge_low[...] = z_courant * low[2] * (from_left[...] - high[...])
    edge_high[...] = -z_courant * high[2] * (from_right[...] - low[...])
    for k in range(2):
        for c in range(comps):
            line_low = jnp.sum(edges[2 * k] * edge_low[c], 0, keepdims=True)
            line_high = jnp.sum(edges[2 * k + 1] * edge_high[c], 0, keepdims=True)
            for t in range(nx // SUB):
                mine = lane % nx == sub + t * SUB
                at_low = jnp.sum(jnp.where(mine, line_low, 0.0), 1, keepdims=True)
                at_high = jnp.sum(jnp.where(mine, line_high, 0.0), 1, keepdims=True)
                add = jnp.where(lane == 0, at_low, jnp.where(lane == LANES - 1, at_high, 0.0))
                put(values, tile(dots, comps * k + c, t=t) + add, comps * k + c, t=t)


def sweep_kernel(rhs, low, high, wid, hid, rec, out, buf_a, buf_b):
    comps, rows, nx, _ = rhs.shape
    tiles = nx // SUB
    group = LANES // nx
    groups = rows // group
    sub = sub_index()
    zero = jnp.zeros((SUB, LANES), f32)
    middle = jnp.zeros((LANES - 2 * SUB, LANES), f32)

    def spread(buf, g):
        for c in range(comps):
            top = jnp.where(sub == 0, low[c, pl.ds(g, 1), :], 0.0)
            bottom = jnp.where(sub == SUB - 1, high[c, pl.ds(g, 1), :], 0.0)
            buf[c] = jnp.concatenate([top, middle, bottom], 0).T

    def process(g, buf, state):
        new = list(state)
        for r in range(group):
            y = g * group + r
            for t in range(tiles):
                r_, h = tile(rec, y, t=t), tile(hid, y, t=t)
                for c in range(comps):
                    k = t * comps + c
                    source = tile(rhs, c, y, t=t) + buf[c, pl.ds(r * nx + t * SUB, SUB), :]
                    new[k] = source * r_ + h * new[k]
                    put(out, new[k], c, y, t=t)
        return tuple(new)

    def forward(m, state):
        g = 2 * m
        spread(buf_b, g + 1)
        state = process(g, buf_a, state)
        spread(buf_a, jnp.minimum(g + 2, groups - 1))
        return process(g + 1, buf_b, state)

    spread(buf_a, 0)
    lax.fori_loop(0, groups // 2, forward, (zero,) * (comps * tiles))

    def backward(k, state):
        y = rows - 1 - k
        new = list(state)
        for t in range(tiles):
            w = tile(wid, y, t=t)
            for c in range(comps):
                k = t * comps + c
                new[k] = tile(out, c, y, t=t) + w * state[k]
                put(out, new[k], c, y, t=t)
        return tuple(new)

    lax.fori_loop(0, rows, backward, (zero,) * (comps * tiles), unroll=4)


def finish_kernel(chunks, part, left, right, flux, out_hbm, out, sems):
    comps, rows, nx, _ = part.shape
    tiles = nx // SUB
    step = rows // chunks

    copies = []
    for k in range(chunks):
        for t in range(tiles):
            fl = [tile(flux, c, t=t) for c in range(comps)]
            fr = [tile(flux, comps + c, t=t) for c in range(comps)]

            def row(y, carry):
                ul, ur = tile(left, y, t=t), tile(right, y, t=t)
                for c in range(comps):
                    put(out, tile(part, c, y, t=t) + (ul * fl[c] + ur * fr[c]), c, y, t=t)
                return carry

            lax.fori_loop(k * step, (k + 1) * step, row, 0, unroll=4)
        span = pl.ds(k * step, step)
        copies.append(pltpu.make_async_copy(out.at[:, span], out_hbm.at[:, span], sems.at[k]))
        copies[-1].start()
    for copy in copies:
        copy.wait()


def vmem_out(*shape):
    return VMEM(shape, f32)


def in_vmem(n):
    return [pl.BlockSpec(memory_space=VMEM)] * n


def cost(flops, moved):
    return pl.CostEstimate(flops=flops, bytes_accessed=moved, transcendentals=0)


def local(velocity, viscosity):
    comps, rows, nx, nz = velocity.shape
    cells = rows * nx * nz
    groups = rows * nx // LANES
    hbm = pl.BlockSpec(memory_space=pltpu.HBM)
    params = pltpu.CompilerParams(vmem_limit_bytes=8 * 2**20)

    wn = lax.axis_index("wn")
    count = lax.axis_size("wn")
    planes = lax.axis_size("xz")
    chip, core = wn // 2, wn % 2
    marks = [
        core == 1,
        wn == 0,
        wn == count - 1,
        (core == 1) == (chip % 2 == 0),
        (chip == 1) | (chip == 2),
    ]
    marks = [jnp.full((1, LANES), 1.0, f32) * mark.astype(f32) for mark in marks]
    marks = jnp.concatenate(marks + [jnp.zeros((SUB - len(marks), LANES), f32)], 0)

    chunk = 16
    vel, low, high, row_out, row_in, wid, hid, rec, fwd, flags = pl.pallas_call(
        functools.partial(head_kernel, chunk),
        out_shape=(
            vmem_out(comps, rows + 2, nx, nz),
            vmem_out(comps, groups, LANES),
            vmem_out(comps, groups, LANES),
            vmem_out(comps + 1, nx, nz),
            vmem_out(comps + 1, nx, nz),
            vmem_out(rows, nx, nz),
            vmem_out(rows, nx, nz),
            vmem_out(rows, nx, nz),
            vmem_out(rows, nx, nz),
            vmem_out(SUB, LANES),
        ),
        in_specs=[hbm, hbm] + in_vmem(1),
        out_specs=in_vmem(10),
        scratch_shapes=[VMEM((rows, nx, nz), f32), pltpu.SemaphoreType.DMA((2, rows // chunk))],
        compiler_params=pltpu.CompilerParams(vmem_limit_bytes=42 * 2**20),
        name="head",
    )(velocity, viscosity, marks)

    with jax.named_scope("halo_z"):
        from_left = lax.ppermute(high, "xz", [(i, (i + 1) % planes) for i in range(planes)])
        from_right = lax.ppermute(low, "xz", [((i + 1) % planes, i) for i in range(planes)])
    with jax.named_scope("halo_y"):
        pairs = [(i, (i + 1) % count if i % 2 else (i - 1) % count) for i in range(count)]
        row_other = lax.ppermute(row_out, "wn", pairs)

    rhs, left, right, ends, dots, edges = pl.pallas_call(
        block_kernel,
        out_shape=(
            vmem_out(comps, rows, nx, nz),
            vmem_out(rows, nx, nz),
            vmem_out(rows, nx, nz),
            vmem_out(3, nx, nz),
            vmem_out(2 * comps, nx, nz),
            vmem_out(4, groups, LANES),
        ),
        in_specs=in_vmem(4),
        out_specs=in_vmem(6),
        scratch_shapes=[VMEM((comps, LANES, LANES), f32)] * 2,
        compiler_params=params,
        cost_estimate=cost(60 * cells, 40 * cells),
        name="block",
    )(vel, wid, rec, fwd)

    edge_low, edge_high, values = pl.pallas_call(
        edge_kernel,
        out_shape=(
            vmem_out(comps, groups, LANES),
            vmem_out(comps, groups, LANES),
            vmem_out(2 * comps, nx, nz),
        ),
        in_specs=in_vmem(6),
        out_specs=in_vmem(3),
        compiler_params=params,
        name="edge",
    )(low, high, from_left, from_right, edges, dots)

    upper_core, first_block, last_block, in_near, middle = (flags[k : k + 1] > 0.5 for k in range(5))
    value_first, value_last = values[:comps], values[comps:]

    cross = ends[1]
    own_out = jnp.where(upper_core, ends[2], ends[0])
    own_in = jnp.where(upper_core, ends[0], ends[2])
    value_out = jnp.where(upper_core, value_last, value_first)
    value_in = jnp.where(upper_core, value_first, value_last)
    sign_in = jnp.where(upper_core, y_courant, -y_courant)
    push_out = jnp.where(first_block | last_block, 0.0, -sign_in * row_out[1] * row_other[:comps])
    face_out = face_rate * (row_out[3] + row_other[3])
    value_out = value_out + own_out * push_out
    value_in = value_in + cross * push_out

    send = jnp.concatenate(
        [jnp.stack([own_out, cross, own_in]), value_out, value_in, row_in, face_out[None]], 0
    )
    with jax.named_scope("exchange_core"):
        got = lax.ppermute(send, "wn", [(i, i ^ 1) for i in range(count)])
    far_out, far_cross, far_in = got[0], got[1], got[2]
    far_value_out, far_value_in = got[3:6], got[6:9]
    far_row, far_face = got[9:13], got[13]
    push_in = sign_in * row_in[1] * far_row[:comps]
    far_push = -sign_in * far_row[1] * row_in[:comps]
    near_value_in = value_in + own_in * push_in
    near_value_out = value_out + cross * push_in
    far_value_out = far_value_out + far_cross * far_push
    far_value_in = far_value_in + far_in * far_push
    join_core = 1.0 / (1.0 / (face_rate * (row_in[3] + far_row[3])) + own_in + far_in)
    flow = join_core * (far_value_in - near_value_in)
    near_near = own_out - cross * cross * join_core
    near_far = cross * far_cross * join_core
    far_far = far_out - far_cross * far_cross * join_core
    near_value = near_value_out + cross * flow
    far_value = far_value_out - far_cross * flow

    chip_in = jnp.where(in_near, near_near, far_far)
    chip_out = jnp.where(in_near, far_far, near_near)
    chip_value_in = jnp.where(in_near, near_value, far_value)
    chip_value_out = jnp.where(in_near, far_value, near_value)
    chip_face_in = jnp.where(in_near, face_out, far_face)
    chip_face_out = jnp.where(in_near, far_face, face_out)
    send = jnp.concatenate(
        [jnp.stack([chip_out, near_far, chip_in, chip_face_out]), chip_value_out, chip_value_in], 0
    )
    with jax.named_scope("exchange_chip"):
        got = lax.ppermute(send, "wn", [(i, i ^ 2) for i in range(count)])

    part = pl.pallas_call(
        sweep_kernel,
        out_shape=vmem_out(comps, rows, nx, nz),
        in_specs=in_vmem(6),
        out_specs=pl.BlockSpec(memory_space=VMEM),
        scratch_shapes=[VMEM((comps, LANES, LANES), f32)] * 2,
        compiler_params=params,
        cost_estimate=cost(30 * cells, 30 * cells),
        name="sweep",
    )(rhs, edge_low, edge_high, wid, hid, rec)

    other_out, other_cross, other_in, other_face = got[0], got[1], got[2], got[3]
    other_value_out, other_value_in = got[4:7], got[7:10]
    join_chip = 1.0 / (1.0 / chip_face_in + chip_in + other_in)
    flow = join_chip * (other_value_in - chip_value_in)
    half_own = jnp.where(
        middle, chip_out - near_far * near_far * join_chip, other_out - other_cross * other_cross * join_chip
    )
    half_value = jnp.where(middle, chip_value_out + near_far * flow, other_value_out - other_cross * flow)
    half_face = jnp.where(middle, chip_face_out, other_face)
    send = jnp.concatenate([half_own[None], half_value], 0)
    with jax.named_scope("exchange_half"):
        got = lax.ppermute(send, "wn", [(i, i ^ 6) for i in range(count)])
    flow_half = (got[1:] - half_value) / (1.0 / half_face + half_own + got[0])

    flow_out = jnp.where(middle, flow_half, 0.0)
    flow_in = join_chip * (
        other_value_in
        - chip_value_in
        + jnp.where(middle, -near_far, other_cross) * flow_half
    )
    flow_near = jnp.where(in_near, flow_in, flow_out)
    flow_far = jnp.where(in_near, flow_out, flow_in)
    flow_core = join_core * (far_value_in + far_cross * flow_far - near_value_in - cross * flow_near)
    total_out = flow_near + push_out
    total_in = flow_core + push_in
    flux = jnp.concatenate(
        [jnp.where(upper_core, total_in, total_out), jnp.where(upper_core, total_out, total_in)], 0
    )

    chunks = 8
    return pl.pallas_call(
        functools.partial(finish_kernel, chunks),
        out_shape=jax.ShapeDtypeStruct((comps, rows, nx, nz), f32),
        in_specs=in_vmem(4),
        out_specs=hbm,
        scratch_shapes=[VMEM((comps, rows, nx, nz), f32), pltpu.SemaphoreType.DMA((chunks,))],
        compiler_params=params,
        name="finish",
    )(part, left, right, flux)


def solution(mesh):
    placed = (P(None, "wn", None, "xz"), P("wn", None, "xz"))
    return jax.shard_map(
        local, mesh=mesh, in_specs=placed, out_specs=P(None, "wn", None, "xz"), check_vma=False
    )
```

time: 284 us -> 37.2 us (0.13); the launches traced: 280 us -> 36.8 us
  other arithmetic: 124 us -> 0.35 us
  blocking collectives: 78 us -> 0 us
  local copies, waits for them, and re-layouts: 61.5 us -> 0.63 us
  Pallas kernels: 0 us -> 17.4 us
  waiting for transfers between devices: 0.01 us -> 5.78 us
    all_gather x6 -> x0, blocking collectives: 78 us -> none  [entering(): everything = jax.tree.map(lambda part: lax.all_gather(part, axis), x)]
    sub x19 -> x0, other arithmetic: 59.8 us -> none  [the longest x1 27 us: advect(): velocity - (x_courant * velocity[0] * diff_x + y_courant * velocity[1] *...]
    unnamed x69 -> x9, other arithmetic: 20 us -> 0.14 us
    slice x6 -> x0, local copies, waits for them, and re-layouts: 18.4 us -> none  [the longest x1 7.02 us: extended(): head = lax.slice_in_dim(cells, 0, width, axis=dim)]
    mul x23 -> x2, other arithmetic: 17.6 us -> 0.01 us  [the longest x1 0.01 us: local(): -sign_in * row_out[1] * row_other[:comps]]
    pallas_call x0 -> x5, Pallas kernels: none -> 17.4 us  [the longest x1 5.91 us: local(): pl.pallas_call(block_kernel, out_shape=(vmem_out(comps, rows, nx, nz), vm...]
    unnamed x321 -> x2, local copies, waits for them, and re-layouts: 16.8 us -> 0.01 us
    ppermute x2 -> x0, local copies, waits for them, and re-layouts: 13.6 us -> none  [the longest x1 6.99 us: extended(): lax.ppermute(head, axis, [((i + 1) % count, i) for i in range(ends)])]
  transfers between devices with their start and end apart: 4 -> 6, of which waited for: 0 -> 2; matrix products, arithmetic and copies ran while one was open for 17% -> 0% of each run, Pallas kernels for 0% -> 26%
where the time goes in v1:
time: 37.2 us; the launch traced here: 36.8 us
  Pallas kernels  17.4 us (47%)
  starting transfers between devices  12.3 us (33%)
  waiting for transfers between devices  5.78 us (16%)
  local copies, waits for them, and re-layouts  0.63 us (2%)
    pallas_call x1, Pallas kernels, local(): pl.pallas_call(block_kernel, out_shape=(vmem_out(comps, rows, nx, nz), vm...  5.91 us
    pallas_call x1, Pallas kernels, local(): pl.pallas_call(functools.partial(head_kernel, chunk), out_shape=(vmem_out...  4.81 us
    ppermute x1, starting transfers between devices, local(): lax.ppermute(low, 'xz', [((i + 1) % planes, i) for i in range(planes)])  4.65 us
    ppermute x1, waiting for transfers between devices, local(): got = lax.ppermute(send, 'wn', [(i, i ^ 2) for i in range(count)])  4.65 us
    pallas_call x1, Pallas kernels, local(): pl.pallas_call(sweep_kernel, out_shape=vmem_out(comps, rows, nx, nz), in_...  3.62 us
    pallas_call x1, Pallas kernels, local(): pl.pallas_call(functools.partial(finish_kernel, chunks), out_shape=jax.Sh...  2.96 us
    ppermute x1, starting transfers between devices, local(): lax.ppermute(high, 'xz', [(i, (i + 1) % planes) for i in range(planes)])  2.54 us
    ppermute x1, starting transfers between devices, local(): row_other = lax.ppermute(row_out, 'wn', pairs)  2.05 us
  transfers between devices with their start and end apart: 6, of which 2 were waited for; matrix products, arithmetic and copies ran while one was open for 0% of the time, Pallas kernels for 26%

profile of v1, /device:TPU:1, one launch (start us, length us, event | category | flops | bytes accessed | tf_op | source)
XLA Modules:
  0.0 36.8 jit_solution(7270857992342539799)
XLA Ops:
  0.0 0.6 %concatenate.15.marks = f32[8,128]{1,0:T(8,128)} concatenate(f32[1,128]{1,0:T(1,128)S(1)} %mul.301, f32[1,128]{1,0:T(1,128)S(1)} %mul.302, f32[1,128]{1,0:T(1,128)S(1)} %mul.303, f32[1,128]{1,0:T(1,128)S(1)} %mul.304, f32[1,128]{1,0:T(1,128)S(1)} %mul.305, f32[3,128]{1,0:T(4,128)S(1)} %broadcast_in_dim.115), dimensions={0} | concatenate | bytes 8192 | tf_op jit(solution)/shard_map/concatenate | solution.py:339
  0.7 4.8 %head.1 = (f32[3,130,32,128]{3,2,1,0:T(8,128)S(1)}, f32[3,32,128]{2,1,0:T(8,128)S(1)}, f32[3,32,128]{2,1,0:T(8,128)S(1)}, f32[4,32,128]{2,1,0:T(8,128)S(1)}, f32...) custom-call(f32[3,128,32,128]{3,2,1,0:T(8,128)} %vel_hbm.1, ...), custom_call_target="tpu_custom_call" | custom-call | tf_op jit(solution)/shard_map/head/pallas_call | solution.py:342
  5.5 2.5 %collective-permute-start = (f32[3,32,128]{2,1,0:T(8,128)S(1)}, f32[3,32,128]{2,1,0:T(8,128)S(1)}, u32[]{:S(2)}, u32[]{:S(2)}) collective-permute-start(f32[3,32,128]{2,1,0:T(8,128)S(1)} %get-tuple-element.30.high), channel_id=1, source_target_pairs={{0,1},{1,2},{2,3},{3,4},{4,5},{5,6},{6,7},{7,8},{8,9},{9,10},{10,1... | collective-permute-start | bytes 147464 | tf_op jit(solution)/shard_map/halo_z/ppermute | solution.py:364
  8.0 4.7 %collective-permute-start.1 = (f32[3,32,128]{2,1,0:T(8,128)S(1)}, f32[3,32,128]{2,1,0:T(8,128)S(1)}, u32[]{:S(2)}, u32[]{:S(2)}) collective-permute-start(f32[3,32,128]{2,1,0:T(8,128)S(1)} %get-tuple-element.29.low), channel_id=1, source_target_pairs={{1,0},{2,1},{3,2},{4,3},{5,4},{6,5},{7,6},{8,7},{9,8},{10,9},{11,1... | collective-permute-start | bytes 147464 | tf_op jit(solution)/shard_map/halo_z/ppermute | solution.py:365
  12.7 2.1 %collective-permute-start.2 = (f32[4,32,128]{2,1,0:T(8,128)S(1)}, f32[4,32,128]{2,1,0:T(8,128)S(1)}, u32[]{:S(2)}, u32[]{:S(2)}) collective-permute-start(f32[4,32,128]{2,1,0:T(8,128)S(1)} %get-tuple-element.42), channel_id=1, source_target_pairs={{0,112},{16,32},{32,16},{48,64},{64,48},{80,96},{96,80},{112,0},{1... | collective-permute-start | bytes 196616 | tf_op jit(solution)/shard_map/halo_y/ppermute | solution.py:368
  14.7 5.9 %block.1 = (f32[3,128,32,128]{3,2,1,0:T(8,128)S(1)}, f32[128,32,128]{2,1,0:T(8,128)S(1)}, f32[128,32,128]{2,1,0:T(8,128)S(1)}, f32[3,32,128]{2,1,0:T(8,128)S(1)}...) custom-call(f32[3,130,32,128]{3,2,1,0:T(8,128)S(1)} %get-tuple-element.24.vel, ...), custom_call_target="tpu_custom_call" | custom-call | flops 31457280 | bytes 20971520 | tf_op jit(solution)/shard_map/block/pallas_call | solution.py:370
  20.7 0.0 collective-permute-done.from_left
  20.7 0.0 collective-permute-done.1.from_right
  20.7 0.1 edge.1
  20.9 0.0 collective-permute-done.2
  21.0 0.9 %collective-permute-start.3 = (f32[14,32,128]{2,1,0:T(8,128)S(1)}, f32[14,32,128]{2,1,0:T(8,128)S(1)}, u32[]{:S(2)}, u32[]{:S(2)}) collective-permute-start(f32[14,32,128]{2,1,0:T(8,128)S(1)} %get-tuple-element.57), channel_id=1, source_target_pairs={{0,16},{16,0},{32,48},{48,32},{64,80},{80,64},{96,112},{112,96},{1... | collective-permute-start | bytes 688136 | tf_op jit(solution)/shard_map/exchange_core/ppermute | solution.py:419
  21.9 1.1 %collective-permute-done.3 = f32[14,32,128]{2,1,0:T(8,128)S(1)} collective-permute-done((f32[14,32,128]{2,1,0:T(8,128)S(1)}, f32[14,32,128]{2,1,0:T(8,128)S(1)}, u32[]{:S(2)}, u32[]{:S(2)}) %collective-permute-start.3) | collective-permute-done | bytes 229408 | tf_op jit(solution)/shard_map/exchange_core/ppermute | solution.py:419
  23.1 0.8 %collective-permute-start.4 = (f32[10,32,128]{2,1,0:T(8,128)S(1)}, f32[10,32,128]{2,1,0:T(8,128)S(1)}, u32[]{:S(2)}, u32[]{:S(2)}) collective-permute-start(f32[10,32,128]{2,1,0:T(8,128)S(1)} %constant_dynamic-update-slice_fusion.7), channel_id=1, source_target_pairs={{0,32},{16,48},{32,0},{48,16},{64,96},{80,112},{96,64},{112,80},{1... | collective-permute-start | bytes 491528 | tf_op jit(solution)/shard_map/exchange_chip/ppermute | solution.py:447
  24.0 4.7 %collective-permute-done.4 = f32[10,32,128]{2,1,0:T(8,128)S(1)} collective-permute-done((f32[10,32,128]{2,1,0:T(8,128)S(1)}, f32[10,32,128]{2,1,0:T(8,128)S(1)}, u32[]{:S(2)}, u32[]{:S(2)}) %collective-permute-start.4) | collective-permute-done | bytes 163872 | tf_op jit(solution)/shard_map/exchange_chip/ppermute | solution.py:447
  28.7 1.3 %collective-permute-start.5 = (f32[4,32,128]{2,1,0:T(8,128)S(1)}, f32[4,32,128]{2,1,0:T(8,128)S(1)}, u32[]{:S(2)}, u32[]{:S(2)}) collective-permute-start(f32[4,32,128]{2,1,0:T(8,128)S(1)} %pad_maximum_fusion.1), channel_id=1, source_target_pairs={{0,96},{16,112},{32,64},{48,80},{64,32},{80,48},{96,0},{112,16},{1... | collective-permute-start | bytes 196616 | tf_op jit(solution)/shard_map/exchange_half/ppermute | solution.py:471
  30.0 3.6 %sweep.1.part = f32[3,128,32,128]{3,2,1,0:T(8,128)S(1)} custom-call(f32[3,128,32,128]{3,2,1,0:T(8,128)S(1)} %get-tuple-element.28.rhs, f32[3,32,128]{2,1,0:T(8,128)S(1)} %get-tuple-element.33.low, f32[3,32,128]{2,1,0:T(8,128)S(1)} %get-tuple-element.34.high, f32[128,32,128]{2,1,0:T(8,128)S(1)} %get-tuple-element.25.wid, ...), custom_call_target="tpu_custom_call" | custom-call | flops 15728640 | bytes 15728640 | tf_op jit(solution)/shard_map/sweep/pallas_call | solution.py:449
  33.7 0.0 collective-permute-done.5
  33.7 0.1 broadcast_select_fusion.3
  33.8 3.0 %finish.1 = f32[3,128,32,128]{3,2,1,0:T(8,128)} custom-call(f32[3,128,32,128]{3,2,1,0:T(8,128)S(1)} %sweep.1.part, f32[128,32,128]{2,1,0:T(8,128)S(1)} %get-tuple-element.36.left, f32[128,32,128]{2,1,0:T(8,128)S(1)} %get-tuple-element.37.right, f32[6,32,128]{2,1,0:T(8,128)S(1)} %pad_maximum_fusion.flux), custom_call_target="tpu_custom_call" | custom-call | tf_op jit(solution)/shard_map/finish/pallas_call | solution.py:490
  (28 shorter events, 0.3 us)
Async XLA Ops:
  5.5 15.2 %collective-permute-start = (f32[3,32,128]{2,1,0:T(8,128)S(1)}, f32[3,32,128]{2,1,0:T(8,128)S(1)}, u32[]{:S(2)}, u32[]{:S(2)}) collective-permute-start(f32[3,32,128]{2,1,0:T(8,128)S(1)} %get-tuple-element.30.high), channel_id=1, source_target_pairs={{0,1},{1,2},{2,3},{3,4},{4,5},{5,6},{6,7},{7,8},{8,9},{9,10},{10,1... | collective-permute-start | bytes 147464 | tf_op jit(solution)/shard_map/halo_z/ppermute | solution.py:364
  8.0 12.7 %collective-permute-start.1 = (f32[3,32,128]{2,1,0:T(8,128)S(1)}, f32[3,32,128]{2,1,0:T(8,128)S(1)}, u32[]{:S(2)}, u32[]{:S(2)}) collective-permute-start(f32[3,32,128]{2,1,0:T(8,128)S(1)} %get-tuple-element.29.low), channel_id=1, source_target_pairs={{1,0},{2,1},{3,2},{4,3},{5,4},{6,5},{7,6},{8,7},{9,8},{10,9},{11,1... | collective-permute-start | bytes 147464 | tf_op jit(solution)/shard_map/halo_z/ppermute | solution.py:365
  12.7 8.2 %collective-permute-start.2 = (f32[4,32,128]{2,1,0:T(8,128)S(1)}, f32[4,32,128]{2,1,0:T(8,128)S(1)}, u32[]{:S(2)}, u32[]{:S(2)}) collective-permute-start(f32[4,32,128]{2,1,0:T(8,128)S(1)} %get-tuple-element.42), channel_id=1, source_target_pairs={{0,112},{16,32},{32,16},{48,64},{64,48},{80,96},{96,80},{112,0},{1... | collective-permute-start | bytes 196616 | tf_op jit(solution)/shard_map/halo_y/ppermute | solution.py:368
  21.0 2.0 %collective-permute-start.3 = (f32[14,32,128]{2,1,0:T(8,128)S(1)}, f32[14,32,128]{2,1,0:T(8,128)S(1)}, u32[]{:S(2)}, u32[]{:S(2)}) collective-permute-start(f32[14,32,128]{2,1,0:T(8,128)S(1)} %get-tuple-element.57), channel_id=1, source_target_pairs={{0,16},{16,0},{32,48},{48,32},{64,80},{80,64},{96,112},{112,96},{1... | collective-permute-start | bytes 688136 | tf_op jit(solution)/shard_map/exchange_core/ppermute | solution.py:419
  23.1 5.5 %collective-permute-start.4 = (f32[10,32,128]{2,1,0:T(8,128)S(1)}, f32[10,32,128]{2,1,0:T(8,128)S(1)}, u32[]{:S(2)}, u32[]{:S(2)}) collective-permute-start(f32[10,32,128]{2,1,0:T(8,128)S(1)} %constant_dynamic-update-slice_fusion.7), channel_id=1, source_target_pairs={{0,32},{16,48},{32,0},{48,16},{64,96},{80,112},{96,64},{112,80},{1... | collective-permute-start | bytes 491528 | tf_op jit(solution)/shard_map/exchange_chip/ppermute | solution.py:447
  28.7 5.0 %collective-permute-start.5 = (f32[4,32,128]{2,1,0:T(8,128)S(1)}, f32[4,32,128]{2,1,0:T(8,128)S(1)}, u32[]{:S(2)}, u32[]{:S(2)}) collective-permute-start(f32[4,32,128]{2,1,0:T(8,128)S(1)} %pad_maximum_fusion.1), channel_id=1, source_target_pairs={{0,96},{16,112},{32,64},{48,80},{64,32},{80,48},{96,0},{112,16},{1... | collective-permute-start | bytes 196616 | tf_op jit(solution)/shard_map/exchange_half/ppermute | solution.py:471

commit v2 on v1

--- a/solution.py
+++ b/solution.py
@@ -40,13 +40,38 @@
     return ref[(*lead, pl.ds(start, rows))].reshape(LANES, LANES)
 
 
+def shifted(ref, lead, t, tiles, forward, sub):
+    if forward:
+        if t < tiles - 1:
+            return ref[(*lead, pl.ds(t * SUB + 1, SUB), slice(None))]
+        mixed = jnp.where(sub == 0, tile(ref, *lead, t=0), tile(ref, *lead, t=t))
+        return pltpu.roll(mixed, SUB - 1, 0)
+    if t > 0:
+        return ref[(*lead, pl.ds(t * SUB - 1, SUB), slice(None))]
+    mixed = jnp.where(sub == SUB - 1, tile(ref, *lead, t=tiles - 1), tile(ref, *lead, t=t))
+    return pltpu.roll(mixed, 1, 0)
+
+
+def shifted(ref, lead, t, tiles, forward, sub):
+    if forward:
+        if t < tiles - 1:
+            return ref[(*lead, pl.ds(t * SUB + 1, SUB), slice(None))]
+        mixed = jnp.where(sub == 0, tile(ref, *lead, t=0), tile(ref, *lead, t=t))
+        return pltpu.roll(mixed, SUB - 1, 0)
+    if t > 0:
+        return ref[(*lead, pl.ds(t * SUB - 1, SUB), slice(None))]
+    mixed = jnp.where(sub == SUB - 1, tile(ref, *lead, t=tiles - 1), tile(ref, *lead, t=t))
+    return pltpu.roll(mixed, 1, 0)
+
+
 def head_kernel(
-    chunk, vel_hbm, visc_hbm, marks, vel, low, high, row_out, row_in, wid, hid, rec, fwd, flags, visc, sems
+    chunk, early, count, vel_hbm, visc_hbm, place, vel, rhs, low, high, row_out, row_in, wid, hid, rec, fwd, flags, visc, sems, *bufs
 ):
     comps, rows, nx, _ = vel_hbm.shape
     tiles = nx // SUB
     group = LANES // nx
     chunks = rows // chunk
+    sub = sub_index()
 
     def visc_copy(k):
         span = pl.ds(k * chunk, chunk)
@@ -57,27 +82,38 @@
         inner = pl.ds(k * chunk + 1, chunk)
         return pltpu.make_async_copy(vel_hbm.at[:, span], vel.at[:, inner], sems.at[1, k])
 
-    for k in range(chunks):
-        visc_copy(k).start()
+    visc_copy(0).start()
     for k in range(chunks):
         vel_copy(k).start()
-    flags[...] = marks[...]
+        if k < chunks - 1:
+            visc_copy(k + 1).start()
+    wn = place[0]
+    core, chip = lax.rem(wn, 2), lax.div(wn, 2)
+    marks = [core == 1, wn == 0, wn == count - 1, core != lax.rem(chip, 2), (chip == 1) | (chip == 2)]
+    marks = [jnp.where(mark, 1.0, 0.0) for mark in marks]
+    table, row = jnp.zeros((SUB, LANES), f32), sub_index()
+    for k, mark in enumerate(marks):
+        table = jnp.where(row == k, mark, table)
+    flags[...] = table
     zero = jnp.zeros((SUB, LANES), f32)
     for c in range(comps):
         for t in range(tiles):
             put(vel, zero, c, 0, t=t)
             put(vel, zero, c, rows + 1, t=t)
-    wall_low = jnp.broadcast_to(marks[1:2, :], (SUB, LANES))
-    wall_high = jnp.broadcast_to(marks[2:3, :], (SUB, LANES))
-
-    def body(k, state, last=False):
-        if not last:
-            visc_copy(k + 1).wait()
-        vel_copy(k).wait()
+    wall_low, wall_high = marks[1], marks[2]
+    central = central_matrix()
+
+    def arrive(g):
+        for c in range(comps):
+            turned = square(vel, c, start=g * group + 1, nx=nx).T
+            low[c, pl.ds(g, 1), :] = turned[:1]
+            high[c, pl.ds(g, 1), :] = turned[LANES - 1 :]
+
+    def factor(start, state, last):
         state = list(state)
-        for r in range(chunk):
-            y = k * chunk + r
-            end = last and r == chunk - 1
+        for r in range(group):
+            y = start + r
+            end = last and r == group - 1
             for t in range(tiles):
                 extra, cell, face, reach = state[4 * t : 4 * t + 4]
                 inner = 1.0 + extra
@@ -96,14 +132,23 @@
                 put(rec, r_, y, t=t)
                 put(fwd, reach, y, t=t)
                 state[4 * t : 4 * t + 4] = [w * inner, next_cell, next_face, reach]
-            if r % group == group - 1:
-                start = k * chunk + r - group + 1
-                spot = (k * chunk + r) // group
-                for c in range(comps):
-                    turned = square(vel, c, start=start + 1, nx=nx).T
-                    low[c, pl.ds(spot, 1), :] = turned[:1]
-                    high[c, pl.ds(spot, 1), :] = turned[LANES - 1 :]
         return tuple(state)
+
+    several = chunk // group
+
+    def body(k, state, sources, first=False, last=False):
+        if not last:
+            visc_copy(k + 1).wait()
+        vel_copy(k).wait()
+        for j in range(several):
+            g = several * k + j
+            arrive(g)
+            state = factor(g * group, state, last and j == several - 1)
+            if sources:
+                if j or not first:
+                    advect(vel, bufs[j - 1], rhs, g - 1)
+                differ(vel, central, bufs[j], g, nx)
+        return state
 
     visc_copy(0).wait()
     state = []
@@ -111,10 +156,30 @@
     for t in range(tiles):
         cell = face_rate * tile(visc, 0, t=t)
         state += [wall_low * (2.0 * cell), cell, one, one]
-    state = lax.fori_loop(0, chunks - 1, body, tuple(state))
-    body(chunks - 1, state, last=True)
-
-    upper = jnp.broadcast_to(marks[0:1, :], (SUB, LANES)) > 0.5
+    split = early // several
+    state = body(0, tuple(state), True, first=True)
+    state = lax.fori_loop(1, split, lambda k, state: body(k, state, True), state)
+    vel_copy(split).wait()
+    advect(vel, bufs[-1], rhs, early - 1)
+
+    def late(k, state):
+        if_first = k > split
+
+        @pl.when(if_first)
+        def _():
+            vel_copy(k).wait()
+
+        visc_copy(k + 1).wait()
+        for j in range(several):
+            g = several * k + j
+            arrive(g)
+            state = factor(g * group, state, False)
+        return state
+
+    state = lax.fori_loop(split, chunks - 1, late, state)
+    body(chunks - 1, state, False, last=True)
+
+    upper = jnp.broadcast_to(marks[0], (SUB, LANES)) > 0.5
     for c in range(comps + 1):
         for t in range(tiles):
             if c < comps:
@@ -125,38 +190,55 @@
             put(row_in, jnp.where(upper, first, end), c, t=t)
 
 
-def shifted(ref, lead, t, tiles, forward, sub):
-    if forward:
-        if t < tiles - 1:
-            return ref[(*lead, pl.ds(t * SUB + 1, SUB), slice(None))]
-        mixed = jnp.where(sub == 0, tile(ref, *lead, t=0), tile(ref, *lead, t=t))
-        return pltpu.roll(mixed, SUB - 1, 0)
-    if t > 0:
-        return ref[(*lead, pl.ds(t * SUB - 1, SUB), slice(None))]
-    mixed = jnp.where(sub == SUB - 1, tile(ref, *lead, t=tiles - 1), tile(ref, *lead, t=t))
-    return pltpu.roll(mixed, 1, 0)
-
-
-def block_kernel(vel, wid, rec, fwd, rhs, left, right, ends, dots, edges, buf_a, buf_b):
+def central_matrix():
+    a = lax.broadcasted_iota(jnp.int32, (2 * LANES, LANES), 0) % LANES
+    b = lax.broadcasted_iota(jnp.int32, (2 * LANES, LANES), 1)
+    ahead = (a == (b + 1) % LANES).astype(f32)
+    behind = (a == (b + LANES - 1) % LANES).astype(f32)
+    return (z_courant * (ahead - behind)).astype(bf16)
+
+
+def differ(vel, central, buf, g, nx):
+    for c in range(buf.shape[0]):
+        whole = square(vel, c, start=g * (LANES // nx) + 1, nx=nx)
+        coarse = whole.astype(bf16)
+        fine = (whole - coarse.astype(f32)).astype(bf16)
+        buf[c] = jnp.dot(jnp.concatenate([coarse, fine], 1), central, preferred_element_type=f32)
+
+
+def advect(vel, buf, rhs, g):
+    comps, rows, nx, _ = rhs.shape
+    tiles = nx // SUB
+    group = LANES // nx
+    sub = sub_index()
+    for t in range(tiles):
+        below = [tile(vel, c, g * group, t=t) for c in range(comps)]
+        mid = [tile(vel, c, g * group + 1, t=t) for c in range(comps)]
+        for r in range(group):
+            y = g * group + r
+            above = [tile(vel, c, y + 2, t=t) for c in range(comps)]
+            rate_x, rate_y = x_courant * mid[0], y_courant * mid[1]
+            for c in range(comps):
+                lead = (c, y + 1)
+                diff_x = shifted(vel, lead, t, tiles, True, sub) - shifted(vel, lead, t, tiles, False, sub)
+                diff_y = above[c] - below[c]
+                diff_z = buf[c, pl.ds(r * nx + t * SUB, SUB), :]
+                put(rhs, mid[c] - (rate_x * diff_x + rate_y * diff_y + mid[2] * diff_z), c, y, t=t)
+            below, mid = mid, above
+
+
+def block_kernel(early, vel, rhs_in, wid, rec, fwd, rhs, left, right, ends, dots, edges, *bufs):
     comps, rows, nx, _ = rhs.shape
     tiles = nx // SUB
     group = LANES // nx
     groups = rows // group
-    sub = sub_index()
-    a = lax.broadcasted_iota(jnp.int32, (2 * LANES, LANES), 0) % LANES
-    b = lax.broadcasted_iota(jnp.int32, (2 * LANES, LANES), 1)
-    ahead = (a == (b + 1) % LANES).astype(f32)
-    behind = (a == (b + LANES - 1) % LANES).astype(f32)
-    central = (z_courant * (ahead - behind)).astype(bf16)
-
-    def differ(buf, g):
-        for c in range(comps):
-            whole = square(vel, c, start=g * group + 1, nx=nx)
-            coarse = whole.astype(bf16)
-            fine = (whole - coarse.astype(f32)).astype(bf16)
-            buf[c] = jnp.dot(jnp.concatenate([coarse, fine], 1), central, preferred_element_type=f32)
-
-    def process(g, buf, state):
+    several = len(bufs)
+    central = central_matrix()
+    side = lax.broadcasted_iota(jnp.int32, (SUB, 2 * LANES), 0)
+    spot = lax.broadcasted_iota(jnp.int32, (SUB, 2 * LANES), 1) % LANES
+    ends_only = (((side == 0) & (spot == 0)) | ((side == 1) & (spot == LANES - 1))).astype(bf16)
+
+    def process(g, state):
         state = list(state)
         for r in reversed(range(group)):
             y = g * group + r
@@ -166,41 +248,49 @@
                 ul, ur = tile(fwd, y, t=t) + w * ul, w * ur
                 put(left, ul, y, t=t)
                 put(right, ur, y, t=t)
-                mid = [tile(vel, c, y + 1, t=t) for c in range(comps)]
-                rate_x, rate_y = x_courant * mid[0], y_courant * mid[1]
                 for c in range(comps):
-                    lead = (c, y + 1)
-                    diff_x = shifted(vel, lead, t, tiles, True, sub) - shifted(vel, lead, t, tiles, False, sub)
-                    diff_y = tile(vel, c, y + 2, t=t) - tile(vel, c, y, t=t)
-                    diff_z = buf[c, pl.ds(r * nx + t * SUB, SUB), :]
-                    source = mid[c] - (rate_x * diff_x + rate_y * diff_y + mid[2] * diff_z)
-                    put(rhs, source, c, y, t=t)
+                    source = tile(rhs, c, y, t=t)
                     sums[c] = sums[c] + ul * source
                     sums[comps + c] = sums[comps + c] + ur * source
                 state[8 * t : 8 * t + 8] = [ul, ur, *sums]
         return tuple(state)
 
     def pack(g):
-        for k, ref in enumerate((left, right)):
-            turned = square(ref, start=g * group, nx=nx).T
-            edges[2 * k, pl.ds(g, 1), :] = turned[:1]
-            edges[2 * k + 1, pl.ds(g, 1), :] = turned[LANES - 1 :]
+        turned = square(left, start=g * group, nx=nx).T
+        edges[0, pl.ds(g, 1), :] = turned[:1]
+        edges[1, pl.ds(g, 1), :] = turned[LANES - 1 :]
+        whole = square(right, start=g * group, nx=nx)
+        coarse = whole.astype(bf16)
+        fine = (whole - coarse.astype(f32)).astype(bf16)
+        picked = lax.dot_general(
+            ends_only, jnp.concatenate([coarse, fine], 1), (((1,), (1,)), ((), ())), preferred_element_type=f32
+        )
+        edges[2, pl.ds(g, 1), :] = picked[:1]
+        edges[3, pl.ds(g, 1), :] = picked[1:2]
+
+    def fresh(m, state):
+        first = groups - 1 - several * m
+        for j in range(several + 1):
+            g = first - j
+            if j < several:
+                differ(vel, central, bufs[j], g, nx)
+            if j:
+                advect(vel, bufs[j - 1], rhs, g + 1)
+                state = process(g + 1, state)
+                pack(g + 1)
+        return state
 
     def body(m, state):
-        g = groups - 1 - 2 * m
-        differ(buf_b, g - 1)
-        state = process(g, buf_a, state)
-        pack(jnp.minimum(g + 1, groups - 1))
-        differ(buf_a, jnp.maximum(g - 2, 0))
-        state = process(g - 1, buf_b, state)
-        pack(g)
+        first = early - 1 - several * m
+        for j in range(several):
+            state = process(first - j, state)
+            pack(first - j)
         return state
 
     zero, one = jnp.zeros((SUB, LANES), f32), jnp.ones((SUB, LANES), f32)
-    differ(buf_a, groups - 1)
     state = ([zero, one] + [zero] * 6) * tiles
-    state = lax.fori_loop(0, groups // 2, body, tuple(state))
-    pack(0)
+    state = lax.fori_loop(0, (groups - early) // several, fresh, tuple(state))
+    state = lax.fori_loop(0, early // several, body, state)
     for t in range(tiles):
         ul, ur, *sums = state[8 * t : 8 * t + 8]
         put(ends, ul, 0, t=t)
@@ -228,7 +318,7 @@
                 put(values, tile(dots, comps * k + c, t=t) + add, comps * k + c, t=t)
 
 
-def sweep_kernel(rhs, low, high, wid, hid, rec, out, buf_a, buf_b):
+def sweep_kernel(rhs, low, high, wid, hid, rec, face, out, face_out, buf_a, buf_b):
     comps, rows, nx, _ = rhs.shape
     tiles = nx // SUB
     group = LANES // nx
@@ -236,6 +326,7 @@
     sub = sub_index()
     zero = jnp.zeros((SUB, LANES), f32)
     middle = jnp.zeros((LANES - 2 * SUB, LANES), f32)
+    face_out[...] = face[...]
 
     def spread(buf, g):
         for c in range(comps):
@@ -327,22 +418,13 @@
     wn = lax.axis_index("wn")
     count = lax.axis_size("wn")
     planes = lax.axis_size("xz")
-    chip, core = wn // 2, wn % 2
-    marks = [
-        core == 1,
-        wn == 0,
-        wn == count - 1,
-        (core == 1) == (chip % 2 == 0),
-        (chip == 1) | (chip == 2),
-    ]
-    marks = [jnp.full((1, LANES), 1.0, f32) * mark.astype(f32) for mark in marks]
-    marks = jnp.concatenate(marks + [jnp.zeros((SUB - len(marks), LANES), f32)], 0)
-
-    chunk = 16
-    vel, low, high, row_out, row_in, wid, hid, rec, fwd, flags = pl.pallas_call(
-        functools.partial(head_kernel, chunk),
+    chunk = 4 * LANES // nx
+    early = 8
+    vel, rhs, low, high, row_out, row_in, wid, hid, rec, fwd, flags = pl.pallas_call(
+        functools.partial(head_kernel, chunk, early, count),
         out_shape=(
             vmem_out(comps, rows + 2, nx, nz),
+            vmem_out(comps, rows, nx, nz),
             vmem_out(comps, groups, LANES),
             vmem_out(comps, groups, LANES),
             vmem_out(comps + 1, nx, nz),
@@ -353,12 +435,16 @@
             vmem_out(rows, nx, nz),
             vmem_out(SUB, LANES),
         ),
-        in_specs=[hbm, hbm] + in_vmem(1),
-        out_specs=in_vmem(10),
-        scratch_shapes=[VMEM((rows, nx, nz), f32), pltpu.SemaphoreType.DMA((2, rows // chunk))],
-        compiler_params=pltpu.CompilerParams(vmem_limit_bytes=42 * 2**20),
+        in_specs=[hbm, hbm, pl.BlockSpec(memory_space=pltpu.SMEM)],
+        out_specs=in_vmem(11),
+        scratch_shapes=[
+            VMEM((rows, nx, nz), f32),
+            pltpu.SemaphoreType.DMA((2, rows // chunk)),
+            *[VMEM((comps, LANES, LANES), f32)] * (chunk * nx // LANES),
+        ],
+        compiler_params=pltpu.CompilerParams(vmem_limit_bytes=39 * 2**20),
         name="head",
-    )(velocity, viscosity, marks)
+    )(velocity, viscosity, wn.astype(jnp.int32).reshape(1))
 
     with jax.named_scope("halo_z"):
         from_left = lax.ppermute(high, "xz", [(i, (i + 1) % planes) for i in range(planes)])
@@ -368,7 +454,7 @@
         row_other = lax.ppermute(row_out, "wn", pairs)
 
     rhs, left, right, ends, dots, edges = pl.pallas_call(
-        block_kernel,
+        functools.partial(block_kernel, early),
         out_shape=(
             vmem_out(comps, rows, nx, nz),
             vmem_out(rows, nx, nz),
@@ -377,13 +463,14 @@
             vmem_out(2 * comps, nx, nz),
             vmem_out(4, groups, LANES),
         ),
-        in_specs=in_vmem(4),
+        in_specs=in_vmem(5),
         out_specs=in_vmem(6),
-        scratch_shapes=[VMEM((comps, LANES, LANES), f32)] * 2,
+        scratch_shapes=[VMEM((comps, LANES, LANES), f32)] * 8,
+        input_output_aliases={1: 0},
         compiler_params=params,
-        cost_estimate=cost(60 * cells, 40 * cells),
+        cost_estimate=cost(40 * cells, 32 * cells),
         name="block",
-    )(vel, wid, rec, fwd)
+    )(vel, rhs, wid, rec, fwd)
 
     edge_low, edge_high, values = pl.pallas_call(
         edge_kernel,
@@ -446,16 +533,16 @@
     with jax.named_scope("exchange_chip"):
         got = lax.ppermute(send, "wn", [(i, i ^ 2) for i in range(count)])
 
-    part = pl.pallas_call(
+    part, chip_face_in = pl.pallas_call(
         sweep_kernel,
-        out_shape=vmem_out(comps, rows, nx, nz),
-        in_specs=in_vmem(6),
-        out_specs=pl.BlockSpec(memory_space=VMEM),
+        out_shape=(vmem_out(comps, rows, nx, nz), vmem_out(nx, nz)),
+        in_specs=in_vmem(7),
+        out_specs=in_vmem(2),
         scratch_shapes=[VMEM((comps, LANES, LANES), f32)] * 2,
         compiler_params=params,
         cost_estimate=cost(30 * cells, 30 * cells),
         name="sweep",
-    )(rhs, edge_low, edge_high, wid, hid, rec)
+    )(rhs, edge_low, edge_high, wid, hid, rec, chip_face_in)
 
     other_out, other_cross, other_in, other_face = got[0], got[1], got[2], got[3]
     other_value_out, other_value_in = got[4:7], got[7:10]

time: 37.2 us -> 35.4 us (0.952)
  the two profiles are of different devices: /device:TPU:1 before, /device:TPU:0 now
where the time goes in v2:
time: 35.4 us; the launch traced here: 35.3 us
  Pallas kernels  15.5 us (44%)
  starting transfers between devices  13 us (37%)
  waiting for transfers between devices  6.16 us (17%)
  other arithmetic  0.39 us (1%)
    ppermute x1, starting transfers between devices, local(): lax.ppermute(low, 'xz', [((i + 1) % planes, i) for i in range(planes)])  6.65 us
    pallas_call x1, Pallas kernels, local(): pl.pallas_call(functools.partial(block_kernel, early), out_shape=(vmem_ou...  4.56 us
    pallas_call x1, Pallas kernels, local(): pl.pallas_call(functools.partial(head_kernel, chunk, early, count), out_s...  4.2 us
    pallas_call x1, Pallas kernels, local(): pl.pallas_call(sweep_kernel, out_shape=(vmem_out(comps, rows, nx, nz), vm...  3.62 us
    pallas_call x1, Pallas kernels, local(): pl.pallas_call(functools.partial(finish_kernel, chunks), out_shape=jax.Sh...  2.96 us
    ppermute x1, starting transfers between devices, local(): got = lax.ppermute(send, 'wn', [(i, i ^ 6) for i in range(count)])  2.82 us
    ppermute x1, waiting for transfers between devices, local(): got = lax.ppermute(send, 'wn', [(i, i ^ 6) for i in range(count)])  2.73 us
    ppermute x1, starting transfers between devices, local(): row_other = lax.ppermute(row_out, 'wn', pairs)  1.91 us
  transfers between devices with their start and end apart: 6, of which 4 were waited for; matrix products, arithmetic and copies ran while one was open for 0% of the time, Pallas kernels for 24%

profile of v2, /device:TPU:0, one launch (start us, length us, event | category | flops | bytes accessed | tf_op | source)
XLA Modules:
  0.0 35.3 jit_solution(2610268291993157468)
XLA Ops:
  0.0 4.2 %head.1 = (f32[3,130,32,128]{3,2,1,0:T(8,128)S(1)}, f32[3,128,32,128]{3,2,1,0:T(8,128)S(1)}, f32[3,32,128]{2,1,0:T(8,128)S(1)}, f32[3,32,128]{2,1,0:T(8,128)S(1)...) custom-call(f32[3,128,32,128]{3,2,1,0:T(8,128)} %vel_hbm.1, ...), custom_call_target="tpu_custom_call" | custom-call | tf_op jit(solution)/shard_map/head/pallas_call | solution.py:423
  4.2 6.7 %collective-permute-start.1 = (f32[3,32,128]{2,1,0:T(8,128)S(1)}, f32[3,32,128]{2,1,0:T(8,128)S(1)}, u32[]{:S(2)}, u32[]{:S(2)}) collective-permute-start(f32[3,32,128]{2,1,0:T(8,128)S(1)} %get-tuple-element.33.low), channel_id=1, source_target_pairs={{1,0},{2,1},{3,2},{4,3},{5,4},{6,5},{7,6},{8,7},{9,8},{10,9},{11,1... | collective-permute-start | bytes 147464 | tf_op jit(solution)/shard_map/halo_z/ppermute | solution.py:451
  10.9 0.0 collective-permute-start
  10.9 1.9 %collective-permute-start.2 = (f32[4,32,128]{2,1,0:T(8,128)S(1)}, f32[4,32,128]{2,1,0:T(8,128)S(1)}, u32[]{:S(2)}, u32[]{:S(2)}) collective-permute-start(f32[4,32,128]{2,1,0:T(8,128)S(1)} %get-tuple-element.41), channel_id=1, source_target_pairs={{0,112},{16,32},{32,16},{48,64},{64,48},{80,96},{96,80},{112,0},{1... | collective-permute-start | bytes 196616 | tf_op jit(solution)/shard_map/halo_y/ppermute | solution.py:454
  12.8 4.6 %block.1 = (f32[3,128,32,128]{3,2,1,0:T(8,128)S(1)}, f32[128,32,128]{2,1,0:T(8,128)S(1)}, f32[128,32,128]{2,1,0:T(8,128)S(1)}, f32[3,32,128]{2,1,0:T(8,128)S(1)}...) custom-call(f32[3,130,32,128]{3,2,1,0:T(8,128)S(1)} %get-tuple-element.27.vel, ...), custom_call_target="tpu_custom_call", output_to_operand_aliasing={{0}: (1, {})} | custom-call | flops 20971520 | bytes 16777216 | tf_op jit(solution)/shard_map/block/pallas_call | solution.py:456
  17.4 0.0 collective-permute-done.1.from_right
  17.4 0.8 %collective-permute-done.from_left = f32[3,32,128]{2,1,0:T(8,128)S(1)} collective-permute-done((f32[3,32,128]{2,1,0:T(8,128)S(1)}, f32[3,32,128]{2,1,0:T(8,128)S(1)}, u32[]{:S(2)}, u32[]{:S(2)}) %collective-permute-start) | collective-permute-done | bytes 49184 | tf_op jit(solution)/shard_map/halo_z/ppermute | solution.py:450
  18.3 0.1 edge.1
  18.4 0.0 collective-permute-done.2
  18.5 0.1 collective-permute-start.3
  18.6 1.5 %collective-permute-done.3 = f32[14,32,128]{2,1,0:T(8,128)S(1)} collective-permute-done((f32[14,32,128]{2,1,0:T(8,128)S(1)}, f32[14,32,128]{2,1,0:T(8,128)S(1)}, u32[]{:S(2)}, u32[]{:S(2)}) %collective-permute-start.3) | collective-permute-done | bytes 229408 | tf_op jit(solution)/shard_map/exchange_core/ppermute | solution.py:506
  20.2 1.6 %collective-permute-start.4 = (f32[10,32,128]{2,1,0:T(8,128)S(1)}, f32[10,32,128]{2,1,0:T(8,128)S(1)}, u32[]{:S(2)}, u32[]{:S(2)}) collective-permute-start(f32[10,32,128]{2,1,0:T(8,128)S(1)} %constant_dynamic-update-slice_fusion.7), channel_id=1, source_target_pairs={{0,32},{16,48},{32,0},{48,16},{64,96},{80,112},{96,64},{112,80},{1... | collective-permute-start | bytes 491528 | tf_op jit(solution)/shard_map/exchange_chip/ppermute | solution.py:534
  21.8 3.6 %sweep.1 = (f32[3,128,32,128]{3,2,1,0:T(8,128)S(1)}, f32[32,128]{1,0:T(8,128)S(1)}) custom-call(f32[3,128,32,128]{3,2,1,0:T(8,128)S(1)} %get-tuple-element.32.rhs, f32[3,32,128]{2,1,0:T(8,128)S(1)} %get-tuple-element.37.low, f32[3,32,128]{2,1,0:T(8,128)S(1)} %get-tuple-element.38.high, f32[128,32,128]{2,1,0:T(8,128)S(1)} %get-tuple-element.29.wid, ...), custom_call_target="tpu_custom_call" | custom-call | flops 15728640 | bytes 15728640 | tf_op jit(solution)/shard_map/sweep/pallas_call | solution.py:536
  25.4 1.1 %collective-permute-done.4 = f32[10,32,128]{2,1,0:T(8,128)S(1)} collective-permute-done((f32[10,32,128]{2,1,0:T(8,128)S(1)}, f32[10,32,128]{2,1,0:T(8,128)S(1)}, u32[]{:S(2)}, u32[]{:S(2)}) %collective-permute-start.4) | collective-permute-done | bytes 163872 | tf_op jit(solution)/shard_map/exchange_chip/ppermute | solution.py:534
  26.6 2.8 %collective-permute-start.5 = (f32[4,32,128]{2,1,0:T(8,128)S(1)}, f32[4,32,128]{2,1,0:T(8,128)S(1)}, u32[]{:S(2)}, u32[]{:S(2)}) collective-permute-start(f32[4,32,128]{2,1,0:T(8,128)S(1)} %pad_maximum_fusion.1), channel_id=1, source_target_pairs={{0,96},{16,112},{32,64},{48,80},{64,32},{80,48},{96,0},{112,16},{1... | collective-permute-start | bytes 196616 | tf_op jit(solution)/shard_map/exchange_half/ppermute | solution.py:558
  29.5 2.7 %collective-permute-done.5 = f32[4,32,128]{2,1,0:T(8,128)S(1)} collective-permute-done((f32[4,32,128]{2,1,0:T(8,128)S(1)}, f32[4,32,128]{2,1,0:T(8,128)S(1)}, u32[]{:S(2)}, u32[]{:S(2)}) %collective-permute-start.5) | collective-permute-done | bytes 65568 | tf_op jit(solution)/shard_map/exchange_half/ppermute | solution.py:558
  32.2 0.1 broadcast_select_fusion.3
  32.3 3.0 %finish.1 = f32[3,128,32,128]{3,2,1,0:T(8,128)} custom-call(f32[3,128,32,128]{3,2,1,0:T(8,128)S(1)} %get-tuple-element.45.part, f32[128,32,128]{2,1,0:T(8,128)S(1)} %get-tuple-element.46.left, f32[128,32,128]{2,1,0:T(8,128)S(1)} %get-tuple-element.47.right, f32[6,32,128]{2,1,0:T(8,128)S(1)} %pad_maximum_fusion.flux), custom_call_target="tpu_custom_call" | custom-call | tf_op jit(solution)/shard_map/finish/pallas_call | solution.py:577
  (24 shorter events, 0.3 us)
Async XLA Ops:
  4.2 13.2 %collective-permute-start.1 = (f32[3,32,128]{2,1,0:T(8,128)S(1)}, f32[3,32,128]{2,1,0:T(8,128)S(1)}, u32[]{:S(2)}, u32[]{:S(2)}) collective-permute-start(f32[3,32,128]{2,1,0:T(8,128)S(1)} %get-tuple-element.33.low), channel_id=1, source_target_pairs={{1,0},{2,1},{3,2},{4,3},{5,4},{6,5},{7,6},{8,7},{9,8},{10,9},{11,1... | collective-permute-start | bytes 147464 | tf_op jit(solution)/shard_map/halo_z/ppermute | solution.py:451
  10.9 7.4 %collective-permute-start = (f32[3,32,128]{2,1,0:T(8,128)S(1)}, f32[3,32,128]{2,1,0:T(8,128)S(1)}, u32[]{:S(2)}, u32[]{:S(2)}) collective-permute-start(f32[3,32,128]{2,1,0:T(8,128)S(1)} %get-tuple-element.34.high), channel_id=1, source_target_pairs={{0,1},{1,2},{2,3},{3,4},{4,5},{5,6},{6,7},{7,8},{8,9},{9,10},{10,1... | collective-permute-start | bytes 147464 | tf_op jit(solution)/shard_map/halo_z/ppermute | solution.py:450
  10.9 7.6 %collective-permute-start.2 = (f32[4,32,128]{2,1,0:T(8,128)S(1)}, f32[4,32,128]{2,1,0:T(8,128)S(1)}, u32[]{:S(2)}, u32[]{:S(2)}) collective-permute-start(f32[4,32,128]{2,1,0:T(8,128)S(1)} %get-tuple-element.41), channel_id=1, source_target_pairs={{0,112},{16,32},{32,16},{48,64},{64,48},{80,96},{96,80},{112,0},{1... | collective-permute-start | bytes 196616 | tf_op jit(solution)/shard_map/halo_y/ppermute | solution.py:454
  18.5 1.6 %collective-permute-start.3 = (f32[14,32,128]{2,1,0:T(8,128)S(1)}, f32[14,32,128]{2,1,0:T(8,128)S(1)}, u32[]{:S(2)}, u32[]{:S(2)}) collective-permute-start(f32[14,32,128]{2,1,0:T(8,128)S(1)} %get-tuple-element.61), channel_id=1, source_target_pairs={{0,16},{16,0},{32,48},{48,32},{64,80},{80,64},{96,112},{112,96},{1... | collective-permute-start | bytes 688136 | tf_op jit(solution)/shard_map/exchange_core/ppermute | solution.py:506
  20.2 6.3 %collective-permute-start.4 = (f32[10,32,128]{2,1,0:T(8,128)S(1)}, f32[10,32,128]{2,1,0:T(8,128)S(1)}, u32[]{:S(2)}, u32[]{:S(2)}) collective-permute-start(f32[10,32,128]{2,1,0:T(8,128)S(1)} %constant_dynamic-update-slice_fusion.7), channel_id=1, source_target_pairs={{0,32},{16,48},{32,0},{48,16},{64,96},{80,112},{96,64},{112,80},{1... | collective-permute-start | bytes 491528 | tf_op jit(solution)/shard_map/exchange_chip/ppermute | solution.py:534
  26.6 5.6 %collective-permute-start.5 = (f32[4,32,128]{2,1,0:T(8,128)S(1)}, f32[4,32,128]{2,1,0:T(8,128)S(1)}, u32[]{:S(2)}, u32[]{:S(2)}) collective-permute-start(f32[4,32,128]{2,1,0:T(8,128)S(1)} %pad_maximum_fusion.1), channel_id=1, source_target_pairs={{0,96},{16,112},{32,64},{48,80},{64,32},{80,48},{96,0},{112,16},{1... | collective-permute-start | bytes 196616 | tf_op jit(solution)/shard_map/exchange_half/ppermute | solution.py:558

commit v3 on v2

--- a/solution.py
+++ b/solution.py
@@ -89,7 +89,7 @@
             visc_copy(k + 1).start()
     wn = place[0]
     core, chip = lax.rem(wn, 2), lax.div(wn, 2)
-    marks = [core == 1, wn == 0, wn == count - 1, core != lax.rem(chip, 2), (chip == 1) | (chip == 2)]
+    marks = [core == 1, wn == 0, wn == count - 1, lax.rem(chip, 2) == 1, chip >= 2]
     marks = [jnp.where(mark, 1.0, 0.0) for mark in marks]
     table, row = jnp.zeros((SUB, LANES), f32), sub_index()
     for k, mark in enumerate(marks):
@@ -485,7 +485,7 @@
         name="edge",
     )(low, high, from_left, from_right, edges, dots)
 
-    upper_core, first_block, last_block, in_near, middle = (flags[k : k + 1] > 0.5 for k in range(5))
+    upper_core, first_block, last_block, odd_chip, high_chip = (flags[k : k + 1] > 0.5 for k in range(5))
     value_first, value_last = values[:comps], values[comps:]
 
     cross = ends[1]
@@ -499,76 +499,96 @@
     value_out = value_out + own_out * push_out
     value_in = value_in + cross * push_out
 
-    send = jnp.concatenate(
-        [jnp.stack([own_out, cross, own_in]), value_out, value_in, row_in, face_out[None]], 0
-    )
+    def mine(part):
+        return jnp.where(upper_core, part[..., nx // 2 :, :], part[..., : nx // 2, :])
+
+    def others(part):
+        return jnp.where(upper_core, part[..., : nx // 2, :], part[..., nx // 2 :, :])
+
+    parts = [own_out[None], cross[None], own_in[None], value_out, value_in, row_in, face_out[None]]
+    send = jnp.concatenate([others(part) for part in parts], 0)
     with jax.named_scope("exchange_core"):
         got = lax.ppermute(send, "wn", [(i, i ^ 1) for i in range(count)])
     far_out, far_cross, far_in = got[0], got[1], got[2]
     far_value_out, far_value_in = got[3:6], got[6:9]
     far_row, far_face = got[9:13], got[13]
-    push_in = sign_in * row_in[1] * far_row[:comps]
-    far_push = -sign_in * far_row[1] * row_in[:comps]
+    own_out, cross, own_in, value_out, value_in, near_row, near_face = map(
+        mine, (own_out, cross, own_in, value_out, value_in, row_in, face_out)
+    )
+    push_in = sign_in * near_row[1] * far_row[:comps]
+    far_push = -sign_in * far_row[1] * near_row[:comps]
     near_value_in = value_in + own_in * push_in
     near_value_out = value_out + cross * push_in
     far_value_out = far_value_out + far_cross * far_push
     far_value_in = far_value_in + far_in * far_push
-    join_core = 1.0 / (1.0 / (face_rate * (row_in[3] + far_row[3])) + own_in + far_in)
+    join_core = 1.0 / (1.0 / (face_rate * (near_row[3] + far_row[3])) + own_in + far_in)
     flow = join_core * (far_value_in - near_value_in)
     near_near = own_out - cross * cross * join_core
-    near_far = cross * far_cross * join_core
     far_far = far_out - far_cross * far_cross * join_core
     near_value = near_value_out + cross * flow
     far_value = far_value_out - far_cross * flow
 
-    chip_in = jnp.where(in_near, near_near, far_far)
-    chip_out = jnp.where(in_near, far_far, near_near)
-    chip_value_in = jnp.where(in_near, near_value, far_value)
-    chip_value_out = jnp.where(in_near, far_value, near_value)
-    chip_face_in = jnp.where(in_near, face_out, far_face)
-    chip_face_out = jnp.where(in_near, far_face, face_out)
+    face_low = jnp.where(upper_core, far_face, near_face)
     send = jnp.concatenate(
-        [jnp.stack([chip_out, near_far, chip_in, chip_face_out]), chip_value_out, chip_value_in], 0
+        [
+            jnp.where(upper_core, far_far, near_near)[None],
+            (cross * far_cross * join_core)[None],
+            jnp.where(upper_core, near_near, far_far)[None],
+            face_low[None],
+            jnp.where(upper_core, far_value, near_value),
+            jnp.where(upper_core, near_value, far_value),
+        ],
+        0,
     )
-    with jax.named_scope("exchange_chip"):
-        got = lax.ppermute(send, "wn", [(i, i ^ 2) for i in range(count)])
-
-    part, chip_face_in = pl.pallas_call(
+    with jax.named_scope("exchange_chips"):
+        chips = [send] + [lax.ppermute(send, "wn", [(i, i ^ (2 * k)) for i in range(count)]) for k in (1, 2, 3)]
+
+    part, token = pl.pallas_call(
         sweep_kernel,
-        out_shape=(vmem_out(comps, rows, nx, nz), vmem_out(nx, nz)),
+        out_shape=(vmem_out(comps, rows, nx, nz), vmem_out(*face_low.shape)),
         in_specs=in_vmem(7),
         out_specs=in_vmem(2),
         scratch_shapes=[VMEM((comps, LANES, LANES), f32)] * 2,
         compiler_params=params,
         cost_estimate=cost(30 * cells, 30 * cells),
         name="sweep",
-    )(rhs, edge_low, edge_high, wid, hid, rec, chip_face_in)
-
-    other_out, other_cross, other_in, other_face = got[0], got[1], got[2], got[3]
-    other_value_out, other_value_in = got[4:7], got[7:10]
-    join_chip = 1.0 / (1.0 / chip_face_in + chip_in + other_in)
-    flow = join_chip * (other_value_in - chip_value_in)
-    half_own = jnp.where(
-        middle, chip_out - near_far * near_far * join_chip, other_out - other_cross * other_cross * join_chip
+    )(rhs, edge_low, edge_high, wid, hid, rec, face_low)
+
+    chips = [jnp.where(odd_chip, chips[k ^ 1], chips[k]) for k in range(4)]
+    chips = [jnp.where(high_chip, chips[k ^ 2], chips[k]) for k in range(4)]
+    low_low = [block[0] for block in chips]
+    low_up = [block[1] for block in chips]
+    up_up = [block[2] for block in chips]
+    resist = [None] + [1.0 / block[3] for block in chips[1:]]
+    at_low = [block[4:7] for block in chips]
+    at_up = [block[7:10] for block in chips]
+    join_01 = 1.0 / (resist[1] + up_up[0] + low_low[1])
+    join_23 = 1.0 / (resist[3] + up_up[2] + low_low[3])
+    step_01 = at_low[1] - at_up[0]
+    step_23 = at_low[3] - at_up[2]
+    join_12 = 1.0 / (
+        resist[2] + up_up[1] - low_up[1] * low_up[1] * join_01 + low_low[2] - low_up[2] * low_up[2] * join_23
     )
-    half_value = jnp.where(middle, chip_value_out + near_far * flow, other_value_out - other_cross * flow)
-    half_face = jnp.where(middle, chip_face_out, other_face)
-    send = jnp.concatenate([half_own[None], half_value], 0)
-    with jax.named_scope("exchange_half"):
-        got = lax.ppermute(send, "wn", [(i, i ^ 6) for i in range(count)])
-    flow_half = (got[1:] - half_value) / (1.0 / half_face + half_own + got[0])
-
-    flow_out = jnp.where(middle, flow_half, 0.0)
-    flow_in = join_chip * (
-        other_value_in
-        - chip_value_in
-        + jnp.where(middle, -near_far, other_cross) * flow_half
+    flow_12 = join_12 * (
+        at_low[2] + low_up[2] * join_23 * step_23 - at_up[1] + low_up[1] * join_01 * step_01
     )
-    flow_near = jnp.where(in_near, flow_in, flow_out)
-    flow_far = jnp.where(in_near, flow_out, flow_in)
+    flow_01 = join_01 * (step_01 + low_up[1] * flow_12)
+    flow_23 = join_23 * (step_23 + low_up[2] * flow_12)
+    flow_up = jnp.where(high_chip, jnp.where(odd_chip, 0.0, flow_23), jnp.where(odd_chip, flow_12, flow_01))
+    flow_low = -jnp.where(high_chip, jnp.where(odd_chip, flow_23, flow_12), jnp.where(odd_chip, flow_01, 0.0))
+    flow_up = jnp.where(token < 0.0, token, flow_up)
+    flow_near = jnp.where(upper_core, flow_up, flow_low)
+    flow_far = jnp.where(upper_core, flow_low, flow_up)
     flow_core = join_core * (far_value_in + far_cross * flow_far - near_value_in - cross * flow_near)
-    total_out = flow_near + push_out
-    total_in = flow_core + push_in
+
+    with jax.named_scope("exchange_flux"):
+        back = lax.ppermute(
+            jnp.concatenate([flow_far, far_push - flow_core], 0), "wn", [(i, i ^ 1) for i in range(count)]
+        )
+    keep = jnp.concatenate([flow_near, push_in + flow_core], 0)
+    whole = jnp.concatenate([jnp.where(upper_core, back, keep), jnp.where(upper_core, keep, back)], 1)
+    total_out = whole[:comps] + push_out
+    total_in = whole[comps:]
     flux = jnp.concatenate(
         [jnp.where(upper_core, total_in, total_out), jnp.where(upper_core, total_out, total_in)], 0
     )

time: 35.4 us -> 35.2 us (level)
  the two profiles are of different devices: /device:TPU:0 before, /device:TPU:1 now
where the time goes in v3:
time: 35.2 us; the launch traced here: 35.1 us
  starting transfers between devices  16.7 us (47%)
  Pallas kernels  15.3 us (43%)
  waiting for transfers between devices  2.41 us (7%)
  other arithmetic  0.37 us (1%)
    ppermute x1, starting transfers between devices, local(): lax.ppermute(low, 'xz', [((i + 1) % planes, i) for i in range(planes)])  7.11 us
    pallas_call x1, Pallas kernels, local(): pl.pallas_call(functools.partial(block_kernel, early), out_shape=(vmem_ou...  4.41 us
    pallas_call x1, Pallas kernels, local(): pl.pallas_call(functools.partial(head_kernel, chunk, early, count), out_s...  4.2 us
    pallas_call x1, Pallas kernels, local(): pl.pallas_call(sweep_kernel, out_shape=(vmem_out(comps, rows, nx, nz), vm...  3.62 us
    ppermute x3, starting transfers between devices, local(): lax.ppermute(send, 'wn', [(i, i ^ 2 * k) for i in range(count)])  3.33 us
    pallas_call x1, Pallas kernels, local(): pl.pallas_call(functools.partial(finish_kernel, chunks), out_shape=jax.Sh...  2.96 us
    ppermute x1, starting transfers between devices, local(): lax.ppermute(jnp.concatenate([flow_far, far_push - flow_core], 0), 'wn',...  2.34 us
    ppermute x1, starting transfers between devices, local(): row_other = lax.ppermute(row_out, 'wn', pairs)  2.05 us
  transfers between devices with their start and end apart: 8, of which 4 were waited for; matrix products, arithmetic and copies ran while one was open for 0% of the time, Pallas kernels for 23%

profile of v3, /device:TPU:1, one launch (start us, length us, event | category | flops | bytes accessed | tf_op | source)
XLA Modules:
  0.0 35.1 jit_solution(10154535409690821628)
XLA Ops:
  0.0 4.2 %head.1 = (f32[3,130,32,128]{3,2,1,0:T(8,128)S(1)}, f32[3,128,32,128]{3,2,1,0:T(8,128)S(1)}, f32[3,32,128]{2,1,0:T(8,128)S(1)}, f32[3,32,128]{2,1,0:T(8,128)S(1)...) custom-call(f32[3,128,32,128]{3,2,1,0:T(8,128)} %vel_hbm.1, ...), custom_call_target="tpu_custom_call" | custom-call | tf_op jit(solution)/shard_map/head/pallas_call | solution.py:423
  4.2 7.1 %collective-permute-start.1 = (f32[3,32,128]{2,1,0:T(8,128)S(1)}, f32[3,32,128]{2,1,0:T(8,128)S(1)}, u32[]{:S(2)}, u32[]{:S(2)}) collective-permute-start(f32[3,32,128]{2,1,0:T(8,128)S(1)} %get-tuple-element.33.low), channel_id=1, source_target_pairs={{1,0},{2,1},{3,2},{4,3},{5,4},{6,5},{7,6},{8,7},{9,8},{10,9},{11,1... | collective-permute-start | bytes 147464 | tf_op jit(solution)/shard_map/halo_z/ppermute | solution.py:451
  11.3 0.0 collective-permute-start
  11.3 2.0 %collective-permute-start.2 = (f32[4,32,128]{2,1,0:T(8,128)S(1)}, f32[4,32,128]{2,1,0:T(8,128)S(1)}, u32[]{:S(2)}, u32[]{:S(2)}) collective-permute-start(f32[4,32,128]{2,1,0:T(8,128)S(1)} %get-tuple-element.43), channel_id=1, source_target_pairs={{0,112},{16,32},{32,16},{48,64},{64,48},{80,96},{96,80},{112,0},{1... | collective-permute-start | bytes 196616 | tf_op jit(solution)/shard_map/halo_y/ppermute | solution.py:454
  13.4 4.4 %block.1 = (f32[3,128,32,128]{3,2,1,0:T(8,128)S(1)}, f32[128,32,128]{2,1,0:T(8,128)S(1)}, f32[128,32,128]{2,1,0:T(8,128)S(1)}, f32[3,32,128]{2,1,0:T(8,128)S(1)}...) custom-call(f32[3,130,32,128]{3,2,1,0:T(8,128)S(1)} %get-tuple-element.27.vel, ...), custom_call_target="tpu_custom_call", output_to_operand_aliasing={{0}: (1, {})} | custom-call | flops 20971520 | bytes 16777216 | tf_op jit(solution)/shard_map/block/pallas_call | solution.py:456
  17.9 0.0 collective-permute-done.1.from_right
  17.9 0.0 collective-permute-done.from_left
  17.9 0.1 edge.1
  18.0 0.0 collective-permute-done.2
  18.1 1.9 %collective-permute-start.3 = (f32[14,16,128]{2,1,0:T(8,128)S(1)}, f32[14,16,128]{2,1,0:T(8,128)S(1)}, u32[]{:S(2)}, u32[]{:S(2)}) collective-permute-start(f32[14,16,128]{2,1,0:T(8,128)S(1)} %constant_dynamic-update-slice_fusion), channel_id=1, source_target_pairs={{0,16},{16,0},{32,48},{48,32},{64,80},{80,64},{96,112},{112,96},{1... | collective-permute-start | bytes 344072 | tf_op jit(solution)/shard_map/exchange_core/ppermute | solution.py:511
  20.0 1.0 %collective-permute-done.3 = f32[14,16,128]{2,1,0:T(8,128)S(1)} collective-permute-done((f32[14,16,128]{2,1,0:T(8,128)S(1)}, f32[14,16,128]{2,1,0:T(8,128)S(1)}, u32[]{:S(2)}, u32[]{:S(2)}) %collective-permute-start.3) | collective-permute-done | bytes 114720 | tf_op jit(solution)/shard_map/exchange_core/ppermute | solution.py:511
  21.1 2.6 %collective-permute-start.6 = (f32[10,16,128]{2,1,0:T(8,128)S(1)}, f32[10,16,128]{2,1,0:T(8,128)S(1)}, u32[]{:S(2)}, u32[]{:S(2)}) collective-permute-start(f32[10,16,128]{2,1,0:T(8,128)S(1)} %constant_dynamic-update-slice_fusion.6), channel_id=1, source_target_pairs={{0,96},{16,112},{32,64},{48,80},{64,32},{80,48},{96,0},{112,16},{1... | collective-permute-start | bytes 245768 | tf_op jit(solution)/shard_map/exchange_chips/ppermute | solution.py:544
  23.7 0.5 %collective-permute-start.5 = (f32[10,16,128]{2,1,0:T(8,128)S(1)}, f32[10,16,128]{2,1,0:T(8,128)S(1)}, u32[]{:S(2)}, u32[]{:S(2)}) collective-permute-start(f32[10,16,128]{2,1,0:T(8,128)S(1)} %constant_dynamic-update-slice_fusion.6), channel_id=1, source_target_pairs={{0,64},{16,80},{32,96},{48,112},{64,0},{80,16},{96,32},{112,48},{1... | collective-permute-start | bytes 245768 | tf_op jit(solution)/shard_map/exchange_chips/ppermute | solution.py:544
  24.2 0.3 collective-permute-start.4
  24.4 3.6 %sweep.1 = (f32[3,128,32,128]{3,2,1,0:T(8,128)S(1)}, f32[16,128]{1,0:T(8,128)S(1)}) custom-call(f32[3,128,32,128]{3,2,1,0:T(8,128)S(1)} %get-tuple-element.32.rhs, f32[3,32,128]{2,1,0:T(8,128)S(1)} %get-tuple-element.37.low, f32[3,32,128]{2,1,0:T(8,128)S(1)} %get-tuple-element.38.high, f32[128,32,128]{2,1,0:T(8,128)S(1)} %get-tuple-element.29.wid, ...), custom_call_target="tpu_custom_call" | custom-call | flops 15728640 | bytes 15728640 | tf_op jit(solution)/shard_map/sweep/pallas_call | solution.py:546
  28.1 0.0 collective-permute-done.6
  28.1 0.4 %collective-permute-done.5 = f32[10,16,128]{2,1,0:T(8,128)S(1)} collective-permute-done((f32[10,16,128]{2,1,0:T(8,128)S(1)}, f32[10,16,128]{2,1,0:T(8,128)S(1)}, u32[]{:S(2)}, u32[]{:S(2)}) %collective-permute-start.5) | collective-permute-done | bytes 81952 | tf_op jit(solution)/shard_map/exchange_chips/ppermute | solution.py:544
  28.5 0.2 collective-permute-done.4
  28.7 0.1 fusion.9
  28.8 2.3 %collective-permute-start.7 = (f32[6,16,128]{2,1,0:T(8,128)S(1)}, f32[6,16,128]{2,1,0:T(8,128)S(1)}, u32[]{:S(2)}, u32[]{:S(2)}) collective-permute-start(f32[6,16,128]{2,1,0:T(8,128)S(1)} %pad_maximum_fusion.2), channel_id=1, source_target_pairs={{0,16},{16,0},{32,48},{48,32},{64,80},{80,64},{96,112},{112,96},{1... | collective-permute-start | bytes 147464 | tf_op jit(solution)/shard_map/exchange_flux/ppermute | solution.py:585
  31.2 0.9 %collective-permute-done.7 = f32[6,16,128]{2,1,0:T(8,128)S(1)} collective-permute-done((f32[6,16,128]{2,1,0:T(8,128)S(1)}, f32[6,16,128]{2,1,0:T(8,128)S(1)}, u32[]{:S(2)}, u32[]{:S(2)}) %collective-permute-start.7) | collective-permute-done | bytes 49184 | tf_op jit(solution)/shard_map/exchange_flux/ppermute | solution.py:585
  32.1 3.0 %finish.1 = f32[3,128,32,128]{3,2,1,0:T(8,128)} custom-call(f32[3,128,32,128]{3,2,1,0:T(8,128)S(1)} %get-tuple-element.45.part, f32[128,32,128]{2,1,0:T(8,128)S(1)} %get-tuple-element.46.left, f32[128,32,128]{2,1,0:T(8,128)S(1)} %get-tuple-element.47.right, f32[6,32,128]{2,1,0:T(8,128)S(1)} %pad_maximum_fusion.flux), custom_call_target="tpu_custom_call" | custom-call | tf_op jit(solution)/shard_map/finish/pallas_call | solution.py:597
  (29 shorter events, 0.3 us)
Async XLA Ops:
  4.2 13.7 %collective-permute-start.1 = (f32[3,32,128]{2,1,0:T(8,128)S(1)}, f32[3,32,128]{2,1,0:T(8,128)S(1)}, u32[]{:S(2)}, u32[]{:S(2)}) collective-permute-start(f32[3,32,128]{2,1,0:T(8,128)S(1)} %get-tuple-element.33.low), channel_id=1, source_target_pairs={{1,0},{2,1},{3,2},{4,3},{5,4},{6,5},{7,6},{8,7},{9,8},{10,9},{11,1... | collective-permute-start | bytes 147464 | tf_op jit(solution)/shard_map/halo_z/ppermute | solution.py:451
  11.3 6.6 %collective-permute-start = (f32[3,32,128]{2,1,0:T(8,128)S(1)}, f32[3,32,128]{2,1,0:T(8,128)S(1)}, u32[]{:S(2)}, u32[]{:S(2)}) collective-permute-start(f32[3,32,128]{2,1,0:T(8,128)S(1)} %get-tuple-element.34.high), channel_id=1, source_target_pairs={{0,1},{1,2},{2,3},{3,4},{4,5},{5,6},{6,7},{7,8},{8,9},{9,10},{10,1... | collective-permute-start | bytes 147464 | tf_op jit(solution)/shard_map/halo_z/ppermute | solution.py:450
  11.3 6.7 %collective-permute-start.2 = (f32[4,32,128]{2,1,0:T(8,128)S(1)}, f32[4,32,128]{2,1,0:T(8,128)S(1)}, u32[]{:S(2)}, u32[]{:S(2)}) collective-permute-start(f32[4,32,128]{2,1,0:T(8,128)S(1)} %get-tuple-element.43), channel_id=1, source_target_pairs={{0,112},{16,32},{32,16},{48,64},{64,48},{80,96},{96,80},{112,0},{1... | collective-permute-start | bytes 196616 | tf_op jit(solution)/shard_map/halo_y/ppermute | solution.py:454
  18.1 2.8 %collective-permute-start.3 = (f32[14,16,128]{2,1,0:T(8,128)S(1)}, f32[14,16,128]{2,1,0:T(8,128)S(1)}, u32[]{:S(2)}, u32[]{:S(2)}) collective-permute-start(f32[14,16,128]{2,1,0:T(8,128)S(1)} %constant_dynamic-update-slice_fusion), channel_id=1, source_target_pairs={{0,16},{16,0},{32,48},{48,32},{64,80},{80,64},{96,112},{112,96},{1... | collective-permute-start | bytes 344072 | tf_op jit(solution)/shard_map/exchange_core/ppermute | solution.py:511
  21.1 7.0 %collective-permute-start.6 = (f32[10,16,128]{2,1,0:T(8,128)S(1)}, f32[10,16,128]{2,1,0:T(8,128)S(1)}, u32[]{:S(2)}, u32[]{:S(2)}) collective-permute-start(f32[10,16,128]{2,1,0:T(8,128)S(1)} %constant_dynamic-update-slice_fusion.6), channel_id=1, source_target_pairs={{0,96},{16,112},{32,64},{48,80},{64,32},{80,48},{96,0},{112,16},{1... | collective-permute-start | bytes 245768 | tf_op jit(solution)/shard_map/exchange_chips/ppermute | solution.py:544
  23.7 4.8 %collective-permute-start.5 = (f32[10,16,128]{2,1,0:T(8,128)S(1)}, f32[10,16,128]{2,1,0:T(8,128)S(1)}, u32[]{:S(2)}, u32[]{:S(2)}) collective-permute-start(f32[10,16,128]{2,1,0:T(8,128)S(1)} %constant_dynamic-update-slice_fusion.6), channel_id=1, source_target_pairs={{0,64},{16,80},{32,96},{48,112},{64,0},{80,16},{96,32},{112,48},{1... | collective-permute-start | bytes 245768 | tf_op jit(solution)/shard_map/exchange_chips/ppermute | solution.py:544
  24.2 4.5 %collective-permute-start.4 = (f32[10,16,128]{2,1,0:T(8,128)S(1)}, f32[10,16,128]{2,1,0:T(8,128)S(1)}, u32[]{:S(2)}, u32[]{:S(2)}) collective-permute-start(f32[10,16,128]{2,1,0:T(8,128)S(1)} %constant_dynamic-update-slice_fusion.6), channel_id=1, source_target_pairs={{0,32},{16,48},{32,0},{48,16},{64,96},{80,112},{96,64},{112,80},{1... | collective-permute-start | bytes 245768 | tf_op jit(solution)/shard_map/exchange_chips/ppermute | solution.py:544
  28.8 3.2 %collective-permute-start.7 = (f32[6,16,128]{2,1,0:T(8,128)S(1)}, f32[6,16,128]{2,1,0:T(8,128)S(1)}, u32[]{:S(2)}, u32[]{:S(2)}) collective-permute-start(f32[6,16,128]{2,1,0:T(8,128)S(1)} %pad_maximum_fusion.2), channel_id=1, source_target_pairs={{0,16},{16,0},{32,48},{48,32},{64,80},{80,64},{96,112},{112,96},{1... | collective-permute-start | bytes 147464 | tf_op jit(solution)/shard_map/exchange_flux/ppermute | solution.py:585
